TPU v7x, 256 devices: a whole 4x4x8 slice. The times are simulated.
256 devices in a mesh: tm: 8 (over z_lo, x), space: 8 (over y, core), dp: 4 (over z_hi).
Axes of the slice: x: 4, y: 4, z: 8 (z_hi: 4, z_lo: 2; z = z_hi * 2 + z_lo), core: 2. Of those that a mesh axis runs over, the one named last changes fastest.
Arguments:
- frames_in: bfloat16 [4, 32, 1536, 640], P('dp', 'tm', 'space'), may hold values from -6 to 6
- w_time: bfloat16 [1920, 640], replicated, may hold values from -0.125 to 0.125
- w_down: bfloat16 [640, 1280], replicated, may hold values from -0.25 to 0.25
- w_query: bfloat16 [1280, 1280], replicated, may hold values from -0.15625 to 0.15625
- w_key: bfloat16 [1280, 1280], replicated, may hold values from -0.15625 to 0.15625
- grad_skip: bfloat16 [4, 32, 1536, 640], P('dp', 'tm', 'space'), may hold values from -6 to 6
- grad_out: bfloat16 [4, 8, 1536, 1280], P('dp', 'tm', 'space'), may hold values from -6 to 6
Outputs:
- input_grad: bfloat16 [4, 32, 1536, 640], P('dp', 'tm', 'space')
- time_weight_grad: float32 [1920, 640], P(('space', 'dp'))
- down_weight_grad: float32 [640, 1280], P(('space', 'dp'))
All inputs are finite; a program needn't handle non-finite values.
Results may differ from a plain program's by a relative error of at most 0.008.
Values may be sent and summed in bfloat16 or wider, within the bound.
A program may use at most 256 MiB of HBM per device.

v0:
```python
import math

import jax
import jax.numpy as jnp
from jax import lax
from jax.sharding import PartitionSpec as P

DH = 64


norm_eps = 1e-06
exact_precision = lax.Precision.HIGHEST


def extended(cells, sides, width):
    for axis, dim in sides:
        count = lax.axis_size(axis)
        ends = count - 1
        head = lax.slice_in_dim(cells, 0, width, axis=dim)
        tail = lax.slice_in_dim(cells, cells.shape[dim] - width, cells.shape[dim], axis=dim)
        cells = jnp.concatenate(
            [
                lax.ppermute(tail, axis, [(i, (i + 1) % count) for i in range(ends)]),
                cells,
                lax.ppermute(head, axis, [((i + 1) % count, i) for i in range(ends)]),
            ],
            axis=dim,
        )
    return cells


def contract_last(left_mat, right_mat):
    return lax.dot_general(
        left_mat, right_mat, (((1,), (1,)), ((), ())), preferred_element_type=jnp.float32
    )


def contract_first(left_mat, right_mat):
    return lax.dot_general(
        left_mat, right_mat, (((0,), (0,)), ((), ())), preferred_element_type=jnp.float32
    )


def head_norm(head_rows):
    factor = lax.rsqrt(jnp.mean(head_rows * head_rows, axis=-1, keepdims=True) + norm_eps)
    return (head_rows * factor, factor)


def coarse_backward(coarse, upstream, w_query, w_key, head_dim, num_rows):
    clip_count, frame_count, pixel_count, coarse_width = coarse.shape
    head_count = coarse_width // head_dim
    shape_heads = (clip_count, frame_count, pixel_count, head_count, head_dim)
    coarse_rows = coarse.reshape(-1, coarse_width)
    queries = jnp.dot(coarse_rows, w_query, preferred_element_type=jnp.float32).reshape(shape_heads)
    key_proj = jnp.dot(coarse_rows, w_key, preferred_element_type=jnp.float32).reshape(shape_heads)
    query_n, query_f = head_norm(queries)
    key_n, key_f = head_norm(key_proj)
    score_scale = 1.0 / math.sqrt(head_dim)
    scores = (
        jnp.einsum("asphd,arphd->aphsr", query_n, key_n, precision=exact_precision) * score_scale
    )
    raised = jnp.exp(scores)
    attn_probs = raised / jnp.sum(raised, axis=-1, keepdims=True)
    value_rows = coarse.astype(jnp.float32).reshape(shape_heads)
    cotangent = upstream.astype(jnp.float32).reshape(shape_heads)
    back_probs = jnp.einsum("asphd,arphd->aphsr", cotangent, value_rows, precision=exact_precision)
    back_scores = attn_probs * (
        back_probs - jnp.sum(attn_probs * back_probs, axis=-1, keepdims=True)
    )
    back_values = jnp.einsum("aphsr,asphd->arphd", attn_probs, cotangent, precision=exact_precision)
    back_kn = (
        jnp.einsum("aphsr,asphd->arphd", back_scores, query_n, precision=exact_precision)
        * score_scale
    )
    back_qn = (
        jnp.einsum("aphsr,arphd->asphd", back_scores, key_n, precision=exact_precision)
        * score_scale
    )
    back_query = (
        query_f * (back_qn - query_n * jnp.mean(back_qn * query_n, axis=-1, keepdims=True))
    ).astype(jnp.bfloat16)
    back_key = (
        key_f * (back_kn - key_n * jnp.mean(back_kn * key_n, axis=-1, keepdims=True))
    ).astype(jnp.bfloat16)
    projected = contract_last(back_query.reshape(-1, coarse_width), w_query) + contract_last(
        back_key.reshape(-1, coarse_width), w_key
    )
    combined = (
        cotangent.reshape(-1, coarse_width) + back_values.reshape(-1, coarse_width) + projected
    )
    return combined.astype(jnp.bfloat16).reshape(clip_count, num_rows, pixel_count, coarse_width)


def shards(frames_in, w_time, w_down, w_query, w_key, grad_skip, grad_out):
    clip_count, frame_count, pixel_count, channels = frames_in.shape
    coarse_width = w_down.shape[1]
    coarse_frames = frame_count // 4
    rows_all = (
        clip_count
        * lax.axis_size("dp")
        * frame_count
        * lax.axis_size("tm")
        * pixel_count
        * lax.axis_size("space")
    )
    grad_scale = 1.0 / math.sqrt(rows_all)
    rimmed = extended(frames_in, (("tm", 1),), 1)
    stacked = jnp.concatenate([rimmed[:, :-2], frames_in, rimmed[:, 2:]], axis=-1).reshape(
        -1, 3 * channels
    )
    pre_act = jnp.dot(stacked, w_time, preferred_element_type=jnp.float32)
    logistic = 1.0 / (1.0 + jnp.exp(-pre_act))
    skip_out = (frames_in.reshape(-1, channels).astype(jnp.float32) + pre_act * logistic).astype(
        jnp.bfloat16
    )
    projected = jnp.dot(skip_out, w_down, preferred_element_type=jnp.float32).reshape(
        clip_count, coarse_frames, 4, pixel_count, coarse_width
    )
    coarse = (0.25 * jnp.sum(projected, axis=2)).astype(jnp.bfloat16)
    coarse_mixed, upstream = (
        lax.all_to_all(coarse, "tm", split_axis=2, concat_axis=1, tiled=True),
        lax.all_to_all(grad_out, "tm", split_axis=2, concat_axis=1, tiled=True),
    )
    back_mixed = coarse_backward(coarse_mixed, upstream, w_query, w_key, DH, coarse_mixed.shape[1])
    back_coarse = lax.all_to_all(back_mixed, "tm", split_axis=1, concat_axis=2, tiled=True)
    spread = contract_last(back_coarse.reshape(-1, coarse_width), w_down).reshape(
        clip_count, coarse_frames, 1, pixel_count, channels
    )
    back_skip = (
        grad_skip.astype(jnp.float32).reshape(clip_count, coarse_frames, 4, pixel_count, channels)
        + 0.25 * spread
    ).reshape(-1, channels)
    back_pre = (back_skip * logistic * (1.0 + pre_act * (1.0 - logistic))).astype(jnp.bfloat16)
    pre_frames = back_pre.reshape(clip_count, frame_count, pixel_count, channels)
    pre_rimmed = extended(pre_frames, (("tm", 1),), 1)
    pre_later = pre_rimmed[:, 2:].reshape(-1, channels)
    pre_earlier = pre_rimmed[:, :-2].reshape(-1, channels)
    input_grad = (
        back_skip
        + contract_last(pre_later, w_time[:channels])
        + contract_last(back_pre, w_time[channels : 2 * channels])
        + contract_last(pre_earlier, w_time[2 * channels :])
    )
    input_grad = input_grad.astype(jnp.bfloat16).reshape(
        clip_count, frame_count, pixel_count, channels
    )
    skip_blocks = skip_out.reshape(clip_count, coarse_frames, 4, pixel_count, channels)
    columns = stacked
    time_part = lax.psum_scatter(
        grad_scale * contract_first(columns, back_pre),
        ("space", "dp"),
        scatter_dimension=0,
        tiled=True,
    )
    columns = skip_blocks
    down_part = lax.psum_scatter(
        0.25
        * grad_scale
        * jnp.einsum("asipc,aspd->cd", columns, back_coarse, preferred_element_type=jnp.float32),
        ("space", "dp"),
        scatter_dimension=0,
        tiled=True,
    )
    time_part, down_part = lax.psum((time_part, down_part), "tm")
    return (input_grad, time_part, down_part)


def solution(mesh):
    in_specs = (
        P("dp", "tm", "space", None),
        P(),
        P(),
        P(),
        P(),
        P("dp", "tm", "space", None),
        P("dp", "tm", "space", None),
    )
    out_specs = (P("dp", "tm", "space", None), P(("space", "dp"), None), P(("space", "dp"), None))
    return jax.shard_map(shards, mesh=mesh, in_specs=in_specs, out_specs=out_specs, check_vma=False)
```

profile of v0, /device:TPU:2, one launch (start us, length us, event | category | flops | bytes accessed | tf_op | source)
XLA Modules:
  0.0 562.2 jit_solution(9811974270023498791)
XLA Ops:
  7.2 2.0 fusion.54
  9.2 3.4 collective-permute-start
  12.6 2.5 collective-permute-start.1
  15.1 2.7 copy.171
  18.3 5.3 reduce.16
  23.7 1.9 reshape.320
  25.6 7.2 %all-to-all-start = ((bf16[8,2,15360]{2,1,0:T(2,128)(2,1)}), bf16[8,2,15360]{2,1,0:T(2,128)(2,1)}, u32[]{:S(2)}, u32[]{:S(2)}) async-start(bf16[8,2,15360]{2,1,0:T(2,128)(2,1)} %reshape.320), calls=%async_computation | async-start | bytes 983040 | tf_op jit(solution)/shard_map/all_to_all | solution.py:122
  32.8 2.0 fusion.2
  35.6 4.0 fusion.6
  39.6 3.7 fusion.55
  43.3 3.4 reduce_sum.72
  49.6 5.3 reduce.15
  55.0 1.9 reshape.318
  56.9 5.9 %all-to-all-start.1 = ((bf16[8,2,15360]{2,1,0:T(2,128)(2,1)}), bf16[8,2,15360]{2,1,0:T(2,128)(2,1)}, u32[]{:S(2)}, u32[]{:S(2)}) async-start(bf16[8,2,15360]{2,1,0:T(2,128)(2,1)} %reshape.318), calls=%async_computation.1 | async-start | bytes 983040 | tf_op jit(solution)/shard_map/all_to_all | solution.py:121
  62.9 3.4 reshape.321
  66.2 4.8 bitcast_reduce_fusion
  71.1 2.6 reshape.298
  73.7 3.4 reshape.319
  77.0 4.8 bitcast_reduce_fusion.1
  81.9 3.0 fusion.45
  84.9 3.0 reshape.295
  87.9 2.4 multiply_reduce_fusion.1
  91.3 2.9 reshape.294
  94.3 4.0 fusion.43
  98.3 3.4 reshape.297
  101.7 2.4 multiply_reduce_fusion
  106.7 2.9 reshape.296
  109.6 2.6 reshape.300
  112.2 3.8 broadcast_multiply_fusion
  116.0 6.1 %fusion.23 = (f32[24,20,8]{2,1,0:T(8,128)S(1)}, f32[24,20,8,8]{2,3,1,0:T(8,128)S(1)}) fusion(f32[8,24,20,64]{3,2,1,0:T(8,128)S(1)} %get-tuple-element.25, f32[8,24,20,64]{3,2,1,0:T(8,128)S(1)} %get-tuple-element.26), kind=kOutput, calls=%fused_computation.41 | convolution fusion | flops 23650560 | bytes 2104320 | tf_op jit(solution)/shard_map/asphd,arphd->aphsr/dot_general | solution.py:60
  122.1 3.6 convolution_bitcast_fusion
  125.7 1.8 fusion.20
  127.5 7.6 %fusion.14 = (f32[8,24,20]{0,2,1:T(8,128)}, f32[24,20,64,8]{2,3,1,0:T(8,128)}) fusion(f32[1,8,24,20,64]{4,3,2,1,0:T(8,128)S(1)} %copy-done.2, f32[8,24,20]{0,2,1:T(8,128)S(1)} %copy-done.20, f32[24,20,8,8]{3,2,1,0:T(8,128)S(1)} %get-tuple-element.20, f32[24,20,8]{2,1,0:T(8,128)S(1)} %get-tuple-element.19, f32[24,20,8]{2,1,0:T(8,128)S(1)} %get-tuple-element.17, ...), kind=kOutput, calls=%fused_computation.24 | convolution fusion | flops 24695040 | bytes 3256320 | tf_op jit(solution)/shard_map/aphsr,asphd->arphd/dot_general | solution.py:72
  135.1 9.1 %fusion.17 = (f32[8,24,20]{0,2,1:T(8,128)}, f32[24,20,64,8]{2,3,1,0:T(8,128)}) fusion(f32[1,8,24,20,64]{4,3,2,1,0:T(8,128)S(1)} %copy-done.1, f32[8,24,20]{0,2,1:T(8,128)S(1)} %copy-done.19, f32[24,20,8,8]{3,2,1,0:T(8,128)S(1)} %get-tuple-element.20, f32[24,20,8]{2,1,0:T(8,128)S(1)} %get-tuple-element.19, f32[24,20,8]{2,1,0:T(8,128)S(1)} %get-tuple-element.17, ...), kind=kOutput, calls=%fused_computation.29 | convolution fusion | flops 24695040 | bytes 3256320 | tf_op jit(solution)/shard_map/aphsr,arphd->asphd/dot_general | solution.py:76
  147.4 3.4 fusion.16
  152.0 2.8 reshape.302
  155.6 3.4 fusion.19
  160.3 2.6 reshape.301
  162.9 3.4 copy.104
  166.3 2.7 reshape.299
  169.0 2.4 fusion.56
  171.5 3.3 fusion.5
  174.7 5.7 %all-to-all-start.2 = ((bf16[1,8,24,1280]{3,2,0,1:T(8,128)(2,1)}), bf16[1,8,24,1280]{3,2,0,1:T(8,128)(2,1)}, u32[]{:S(2)}, u32[]{:S(2)}) async-start(bf16[1,8,24,1280]{3,2,0,1:T(8,128)(2,1)} %bitcast.133), calls=%async_computation.2 | async-start | bytes 983040 | tf_op jit(solution)/shard_map/all_to_all | solution.py:125
  183.0 4.0 all-to-all-done.2
  187.0 2.4 convolution_multiply_fusion.2
  189.4 2.6 fusion.10
  192.0 4.7 convolution_multiply_fusion.1
  196.7 3.4 convolution_multiply_fusion
  200.2 206.9 %fusion.52 = (f32[64,640]{1,0:T(8,128)S(1)}, f32[24,1280]{1,0:T(8,128)}) fusion(f32[1920,640]{1,0:T(8,128)} %convolution_multiply_fusion.1, f32[640,1280]{1,0:T(8,128)} %convolution_multiply_fusion), kind=kCustom, calls=%all-reduce-scatter.2 | all-reduce-scatter fusion | flops 2293762 | bytes 8479744
  407.9 2.8 collective-permute-start.11
  410.7 3.8 fusion.34
  414.5 5.9 %collective-permute-start.10 = (f32[24,1280]{1,0:T(8,128)S(1)}, f32[24,1280]{1,0:T(8,128)S(1)}, u32[]{:S(2)}, u32[]{:S(2)}) collective-permute-start(f32[24,1280]{1,0:T(8,128)S(1)} %copy-done.24), channel_id=1, source_target_pairs={{0,5},{1,6},{2,7},{3,8},{4,9},{5,10},{6,11},{7,12},{8,13},{9,14},{... | collective-permute-start | bytes 368648
  421.7 6.0 %collective-permute-start.8 = (f32[24,1280]{1,0:T(8,128)S(1)}, f32[24,1280]{1,0:T(8,128)S(1)}, u32[]{:S(2)}, u32[]{:S(2)}) collective-permute-start(f32[24,1280]{1,0:T(8,128)S(1)} %copy-done.24), channel_id=1, source_target_pairs={{0,3},{1,4},{2,5},{3,6},{4,7},{5,8},{6,9},{7,10},{8,11},{9,12},{10... | collective-permute-start | bytes 368648
  427.7 5.4 collective-permute-start.7
  433.8 2.5 collective-permute-start.6
  437.2 4.8 collective-permute-start.4
  442.0 1.9 collective-permute-start.3
  443.9 10.3 %collective-permute-start.2 = (bf16[1,1,192,640]{3,2,1,0:T(8,128)(2,1)}, bf16[1,1,192,640]{3,2,1,0:T(8,128)(2,1)}, u32[]{:S(2)}, u32[]{:S(2)}) collective-permute-start(bf16[1,1,192,640]{3,2,1,0:T(8,128)(2,1)} %get-tuple-element.12), channel_id=1, source_target_pairs={{32,0},{64,32},{96,64},{128,96},{160,128},{192,160},{224,192},{33,... | collective-permute-start | bytes 737288 | tf_op jit(solution)/shard_map/ppermute | solution.py:25
  454.3 4.2 collective-permute-start.5
  458.5 10.4 %concatenate.23 = f32[148,1280]{1,0:T(8,128)} concatenate(f32[4,1280]{1,0:T(4,128)S(1)} %collective-permute-done.11, f32[24,1280]{1,0:T(8,128)} %copy-done.25, f32[24,1280]{1,0:T(8,128)} %copy-done.26, f32[24,1280]{1,0:T(8,128)} %copy-done.27, f32[24,1280]{1,0:T(8,128)} %copy-done.28, f32[24,1280]{1,0:T(8,128)} %collective-permute-done.6, f32[24,1280]{1,0:T(8,128)} %get-tuple-element.8), dimensions={0} | concatenate | bytes 1515520
  470.5 4.7 concatenate.22
  476.8 1.8 pad_maximum_fusion.2
  480.7 2.0 fusion.13
  482.7 69.2 %all-reduce.8.cloned.1.call-done = (f32[60,640]{1,0:T(8,128)}, f32[20,1280]{1,0:T(8,128)}) async-done(((f32[60,640]{1,0:T(8,128)}, f32[20,1280]{1,0:T(8,128)}), (f32[60,640]{1,0:T(8,128)}, f32[20,1280]{1,0:T(8,128)})) %all-reduce.8.cloned.1.call-update) | async-done | bytes 256016 | tf_op jit(solution)/shard_map/psum | solution.py:164
  (106 shorter events, 28.5 us)
Async XLA Ops:
  7.2 74.7 %copy-start = (bf16[1280,1280]{1,0:T(8,128)(2,1)S(1)}, bf16[1280,1280]{1,0:T(8,128)(2,1)}, u32[]{:S(2)}) copy-start(bf16[1280,1280]{1,0:T(8,128)(2,1)} %param.10) | copy-start | bytes 9830404
  9.2 23.6 %collective-permute-start = (bf16[1,1,192,640]{3,2,1,0:T(8,128)(2,1)}, bf16[1,1,192,640]{3,2,1,0:T(8,128)(2,1)S(1)}, u32[]{:S(2)}, u32[]{:S(2)}) collective-permute-start(bf16[1,1,192,640]{3,2,1,0:T(8,128)(2,1)} %get-tuple-element.13), channel_id=1, source_target_pairs={{0,32},{32,64},{64,96},{96,128},{128,160},{160,192},{192,224},{1,3... | collective-permute-start | bytes 737288 | tf_op jit(solution)/shard_map/ppermute | solution.py:23
  12.6 20.2 %collective-permute-start.1 = (bf16[1,1,192,640]{3,2,1,0:T(8,128)(2,1)}, bf16[1,1,192,640]{3,2,1,0:T(8,128)(2,1)}, u32[]{:S(2)}, u32[]{:S(2)}) collective-permute-start(bf16[1,1,192,640]{3,2,1,0:T(8,128)(2,1)} %get-tuple-element.14), channel_id=1, source_target_pairs={{32,0},{64,32},{96,64},{128,96},{160,128},{192,160},{224,192},{33,... | collective-permute-start | bytes 737288 | tf_op jit(solution)/shard_map/ppermute | solution.py:25
  25.6 31.3 %all-to-all-start = ((bf16[8,2,15360]{2,1,0:T(2,128)(2,1)}), bf16[8,2,15360]{2,1,0:T(2,128)(2,1)}, u32[]{:S(2)}, u32[]{:S(2)}) async-start(bf16[8,2,15360]{2,1,0:T(2,128)(2,1)} %reshape.320), calls=%async_computation | async-start | bytes 983040 | tf_op jit(solution)/shard_map/all_to_all | solution.py:122
  32.8 2.5 copy-start.14
  32.8 2.8 copy-start.16
  34.9 4.7 copy-start.12
  35.6 4.0 copy-start.18
  39.5 3.7 copy-start.23
  56.9 16.7 %all-to-all-start.1 = ((bf16[8,2,15360]{2,1,0:T(2,128)(2,1)}), bf16[8,2,15360]{2,1,0:T(2,128)(2,1)}, u32[]{:S(2)}, u32[]{:S(2)}) async-start(bf16[8,2,15360]{2,1,0:T(2,128)(2,1)} %reshape.318), calls=%async_computation.1 | async-start | bytes 983040 | tf_op jit(solution)/shard_map/all_to_all | solution.py:121
  116.0 6.1 %copy-start.21 = (bf16[8,24,20,64]{3,2,1,0:T(8,128)(2,1)S(1)}, bf16[8,24,20,64]{3,2,1,0:T(8,128)(2,1)}, u32[]{:S(2)}) copy-start(bf16[8,24,20,64]{3,2,1,0:T(8,128)(2,1)} %reshape.298) | copy-start | bytes 1474564
  122.1 3.6 copy-start.22
  125.7 1.8 copy-start.2
  125.7 1.8 copy-start.20
  127.5 7.6 %copy-start.1 = (f32[1,8,24,20,64]{4,3,2,1,0:T(8,128)S(1)}, f32[1,8,24,20,64]{4,3,2,1,0:T(8,128)}, u32[]{:S(2)}) copy-start(f32[1,8,24,20,64]{4,3,2,1,0:T(8,128)} %reshape.295) | copy-start | bytes 2949124
  127.5 7.6 %copy-start.19 = (f32[8,24,20]{0,2,1:T(8,128)S(1)}, f32[8,24,20]{0,2,1:T(8,128)}, u32[]{:S(2)}) copy-start(f32[8,24,20]{0,2,1:T(8,128)} %copy.105) | copy-start | bytes 46084
  169.0 2.4 copy-start.3
  169.0 2.4 copy-start.7
  169.0 2.5 copy-start.17
  171.5 9.0 %copy-start.29 = (u32[256]{0:T(256)S(1)}, u32[256]{0:T(256)}, u32[]{:S(2)}) copy-start(u32[256]{0:T(256)} %constant.27) | copy-start | bytes 3076
  174.7 12.3 %all-to-all-start.2 = ((bf16[1,8,24,1280]{3,2,0,1:T(8,128)(2,1)}), bf16[1,8,24,1280]{3,2,0,1:T(8,128)(2,1)}, u32[]{:S(2)}, u32[]{:S(2)}) async-start(bf16[1,8,24,1280]{3,2,0,1:T(8,128)(2,1)} %bitcast.133), calls=%async_computation.2 | async-start | bytes 983040 | tf_op jit(solution)/shard_map/all_to_all | solution.py:125
  180.4 371.5 %all-reduce.8.cloned.1.call-start = ((), (), s32[]{:S(2)}) async-start(), calls=%async_computation.3 | async-start | bytes 573440 | tf_op jit(solution)/shard_map/psum | solution.py:164
  187.0 2.4 copy-start.10
  189.4 2.6 copy-start.8
  189.4 2.6 copy-start.13
  192.0 4.8 copy-start.4
  407.1 7.4 %copy-start.24 = (f32[24,1280]{1,0:T(8,128)S(1)}, f32[24,1280]{1,0:T(8,128)}, u32[]{:S(2)}) copy-start(f32[24,1280]{1,0:T(8,128)} %get-tuple-element.8) | copy-start | bytes 368644
  407.9 28.4 %copy-start.5 = (bf16[768,640]{1,0:T(8,128)(2,1)S(1)}, bf16[768,640]{1,0:T(8,128)(2,1)}, u32[]{:S(2)}) copy-start(bf16[768,640]{1,0:T(8,128)(2,1)} %copy-done.4) | copy-start | bytes 2949124
  407.9 25.9 %collective-permute-start.11 = (f32[4,1280]{1,0:T(4,128)S(1)}, f32[4,1280]{1,0:T(4,128)S(1)}, u32[]{:S(2)}, u32[]{:S(2)}) collective-permute-start(f32[4,1280]{1,0:T(4,128)S(1)} %slice.51), channel_id=1, source_target_pairs={{0,6},{1,7},{2,8},{3,9},{4,10},{5,11},{6,12},{7,13},{8,14},{9,15},... | collective-permute-start | bytes 61448
  414.5 22.7 %collective-permute-start.10 = (f32[24,1280]{1,0:T(8,128)S(1)}, f32[24,1280]{1,0:T(8,128)S(1)}, u32[]{:S(2)}, u32[]{:S(2)}) collective-permute-start(f32[24,1280]{1,0:T(8,128)S(1)} %copy-done.24), channel_id=1, source_target_pairs={{0,5},{1,6},{2,7},{3,8},{4,9},{5,10},{6,11},{7,12},{8,13},{9,14},{... | collective-permute-start | bytes 368648
  420.4 21.6 %collective-permute-start.9 = (f32[24,1280]{1,0:T(8,128)S(1)}, f32[24,1280]{1,0:T(8,128)S(1)}, u32[]{:S(2)}, u32[]{:S(2)}) collective-permute-start(f32[24,1280]{1,0:T(8,128)S(1)} %copy-done.24), channel_id=1, source_target_pairs={{0,4},{1,5},{2,6},{3,7},{4,8},{5,9},{6,10},{7,11},{8,12},{9,13},{1... | collective-permute-start | bytes 368648
  421.7 22.2 %collective-permute-start.8 = (f32[24,1280]{1,0:T(8,128)S(1)}, f32[24,1280]{1,0:T(8,128)S(1)}, u32[]{:S(2)}, u32[]{:S(2)}) collective-permute-start(f32[24,1280]{1,0:T(8,128)S(1)} %copy-done.24), channel_id=1, source_target_pairs={{0,3},{1,4},{2,5},{3,6},{4,7},{5,8},{6,9},{7,10},{8,11},{9,12},{10... | collective-permute-start | bytes 368648
  427.7 26.5 %collective-permute-start.7 = (f32[24,1280]{1,0:T(8,128)S(1)}, f32[24,1280]{1,0:T(8,128)S(1)}, u32[]{:S(2)}, u32[]{:S(2)}) collective-permute-start(f32[24,1280]{1,0:T(8,128)S(1)} %copy-done.24), channel_id=1, source_target_pairs={{0,2},{1,3},{2,4},{3,5},{4,6},{5,7},{6,8},{7,9},{8,10},{9,11},{10,... | collective-permute-start | bytes 368648
  433.8 24.7 %collective-permute-start.6 = (f32[24,1280]{1,0:T(8,128)S(1)}, f32[24,1280]{1,0:T(8,128)}, u32[]{:S(2)}, u32[]{:S(2)}) collective-permute-start(f32[24,1280]{1,0:T(8,128)S(1)} %copy-done.24), channel_id=1, source_target_pairs={{0,1},{1,2},{2,3},{3,4},{4,5},{5,6},{6,7},{7,8},{8,9},{9,10},{10,1... | collective-permute-start | bytes 368648
  437.2 17.1 %copy-start.25 = (f32[24,1280]{1,0:T(8,128)}, f32[24,1280]{1,0:T(8,128)S(1)}, u32[]{:S(2)}) copy-start(f32[24,1280]{1,0:T(8,128)S(1)} %collective-permute-done.10) | copy-start | bytes 368644
  437.2 33.3 %collective-permute-start.4 = (f32[64,640]{1,0:T(8,128)S(1)}, f32[64,640]{1,0:T(8,128)}, u32[]{:S(2)}, u32[]{:S(2)}) collective-permute-start(f32[64,640]{1,0:T(8,128)S(1)} %get-tuple-element.7), channel_id=1, source_target_pairs={{0,1},{1,2},{2,3},{3,4},{4,5},{5,6},{6,7},{7,8},{8,9},{9,10},{10,1... | collective-permute-start | bytes 491528
  442.0 16.5 %copy-start.26 = (f32[24,1280]{1,0:T(8,128)}, f32[24,1280]{1,0:T(8,128)S(1)}, u32[]{:S(2)}) copy-start(f32[24,1280]{1,0:T(8,128)S(1)} %collective-permute-done.9) | copy-start | bytes 368644
  442.0 34.8 %collective-permute-start.3 = (bf16[1,1,192,640]{3,2,1,0:T(8,128)(2,1)}, bf16[1,1,192,640]{3,2,1,0:T(8,128)(2,1)}, u32[]{:S(2)}, u32[]{:S(2)}) collective-permute-start(bf16[1,1,192,640]{3,2,1,0:T(8,128)(2,1)} %get-tuple-element.11), channel_id=1, source_target_pairs={{0,32},{32,64},{64,96},{96,128},{128,160},{160,192},{192,224},{1,3... | collective-permute-start | bytes 737288 | tf_op jit(solution)/shard_map/ppermute | solution.py:23
  443.9 14.6 %copy-start.27 = (f32[24,1280]{1,0:T(8,128)}, f32[24,1280]{1,0:T(8,128)S(1)}, u32[]{:S(2)}) copy-start(f32[24,1280]{1,0:T(8,128)S(1)} %collective-permute-done.8) | copy-start | bytes 368644
  443.9 32.9 %collective-permute-start.2 = (bf16[1,1,192,640]{3,2,1,0:T(8,128)(2,1)}, bf16[1,1,192,640]{3,2,1,0:T(8,128)(2,1)}, u32[]{:S(2)}, u32[]{:S(2)}) collective-permute-start(bf16[1,1,192,640]{3,2,1,0:T(8,128)(2,1)} %get-tuple-element.12), channel_id=1, source_target_pairs={{32,0},{64,32},{96,64},{128,96},{160,128},{192,160},{224,192},{33,... | collective-permute-start | bytes 737288 | tf_op jit(solution)/shard_map/ppermute | solution.py:25
  454.3 4.2 copy-start.28
  454.3 16.1 %collective-permute-start.5 = (f32[60,640]{1,0:T(8,128)}, f32[60,640]{1,0:T(8,128)}, u32[]{:S(2)}, u32[]{:S(2)}) collective-permute-start(f32[60,640]{1,0:T(8,128)} %slice.50), channel_id=1, source_target_pairs={{0,2},{1,3},{2,4},{3,5},{4,6},{5,7},{6,8},{7,9},{8,10},{9,11},{10,... | collective-permute-start | bytes 460808
  476.8 2.3 copy-start.15
  478.6 1.7 copy-start.6
  478.7 1.7 copy-start.9
  478.7 2.0 copy-start.11
Sparse Core Ops, SparseCore 0:
  476.9 74.9 all-reduce.7
where the time goes:
time: 568 us; the launch traced here: 562 us
  blocking collectives  207 us (36%)
  local copies, waits for them, and re-layouts  91.6 us (16%)
  waiting for transfers between devices  73.2 us (13%)
  starting transfers between devices  69.8 us (12%)
  matrix products  65.9 us (12%)
  other arithmetic  39.2 us (7%)
  between operations  15.4 us (3%)
    unnamed x1, blocking collectives  207 us
    psum x1, waiting for transfers between devices, shards(): time_part, down_part = lax.psum((time_part, down_part), 'tm')  69.2 us
    unnamed x75, local copies, waits for them, and re-layouts  39.2 us
    unnamed x8, starting transfers between devices  32.9 us
    dot_general x6, matrix products, contract_last(): lax.dot_general(left_mat, right_mat, (((1,), (1,)), ((), ())), preferred_...  14.9 us
    ppermute x2, starting transfers between devices, extended(): lax.ppermute(head, axis, [((i + 1) % count, i) for i in range(ends)])  12.8 us
  transfers between devices with their start and end apart: 16, of which 2 were waited for; matrix products, arithmetic and copies ran while one was open for 13% of the time, Pallas kernels for 0%

commit v1 on v0

v1 whole, which is shorter than its diff:
```python
import math

import jax
import jax.numpy as jnp
from jax import lax
from jax.experimental import pallas as pl
from jax.experimental.pallas import tpu as pltpu
from jax.sharding import PartitionSpec as P

C1, C2, DH = 640, 1280, 64
TM, YS, XS, DP = 8, 4, 4, 4
FINE, PIX = 4, 192
OWN = PIX // TM
ROWS_ALL = 4 * 32 * 1536
EPS = 1e-06
MESH = pl.DeviceIdType.MESH
F32, BF16 = jnp.float32, jnp.bfloat16
COLS_FINE = ((0, 256), (256, 512), (512, 640))
COLS_COARSE = tuple((n, n + 256) for n in range(0, C2, 256))


def dot(left, right):
    return jnp.dot(left, right, preferred_element_type=F32)


def dot_last(left, right):
    return lax.dot_general(left, right, (((1,), (1,)), ((), ())), preferred_element_type=F32)


def dot_first(left, right):
    return lax.dot_general(left, right, (((0,), (0,)), ((), ())), preferred_element_type=F32)


def fold_tail(tail):
    return jnp.concatenate([tail[:, :C1], tail[:, C1:]], axis=0)


def open_tail(tail):
    return jnp.concatenate([tail[:8], tail[8:]], axis=1)


class Ring:
    def __init__(self, remote, parts, bufs, pos, plus, minus, first):
        self.parts, self.pos = parts, pos
        self.ra, self.rb, self.fp, self.fm = bufs
        lo, hi = pl.ds(0, 2), pl.ds(2, 2)
        self.ahead, self.behind, far = (pos + 1) % 4, (pos + 3) % 4, (pos + 2) % 4
        self.copies = [
            remote(parts.at[far, lo], self.ra, first, plus),
            remote(parts.at[far, hi], self.rb, first + 1, minus),
            remote(parts.at[self.ahead, hi], self.fp.at[hi], first + 2, plus),
            remote(parts.at[self.behind, lo], self.fm.at[lo], first + 3, minus),
            remote(parts.at[self.ahead, lo], self.fp.at[lo], first + 4, plus),
            remote(parts.at[self.behind, hi], self.fm.at[hi], first + 5, minus),
        ]

    def start(self):
        for copy in self.copies[:4]:
            copy.start()

    def middle(self):
        parts = self.parts
        self.copies[0].wait_recv()
        parts[self.ahead, 0:2] = (parts[self.ahead, 0:2].astype(F32) + self.ra[...].astype(F32)).astype(BF16)
        self.copies[4].start()
        self.copies[1].wait_recv()
        parts[self.behind, 2:4] = (parts[self.behind, 2:4].astype(F32) + self.rb[...].astype(F32)).astype(BF16)
        self.copies[5].start()

    def arrived(self):
        for copy in self.copies[2:]:
            copy.wait_recv()

    def total(self, i):
        return self.parts[self.pos, i].astype(F32) + self.fp[i].astype(F32) + self.fm[i].astype(F32)

    def finish(self):
        for copy in self.copies:
            copy.wait_send()


def kernel(
    frames, w_time, w_down, w_query, w_key, grad_skip, grad_out,
    ig_out, time_out, down_out,
    ext, wt, wd, wq, wk, gs, go, pre, skipsum, work, qf, kf, cb, gb, bq, bk,
    g_send, g_recv, c_send, c_recv, b_send, b_recv, bc, spread, bpe,
    t_sum, d_sum, cs_y, cs_x, p_y, p_x, y_ra, y_rb, y_fp, y_fm, x_ra, x_rb, x_fp, x_fm,
    p2_y, p2_x, y2_ra, y2_rb, y2_fp, y2_fm, x2_ra, x2_rb, x2_fp, x2_fm,
    z_buf, z_recv, w_buf, w_recv, final,
    local_sem, send_sem, recv_sem,
):
    tm, space, dp = lax.axis_index("tm"), lax.axis_index("space"), lax.axis_index("dp")
    core, y, zlo, x = space % 2, space // 2, tm // XS, tm % XS

    def at(tm_=None, space_=None, dp_=None):
        return {
            "tm": tm if tm_ is None else tm_,
            "space": space if space_ is None else space_,
            "dp": dp if dp_ is None else dp_,
        }

    loads = [
        pltpu.make_async_copy(src, dst, local_sem.at[i])
        for i, (src, dst) in enumerate(
            (
                (frames.at[0], ext.at[pl.ds(1, FINE)]),
                (w_time, wt),
                (grad_out.at[0, 0], go),
                (w_down, wd),
                (w_query, wq),
                (w_key, wk),
                (grad_skip.at[0], gs),
            )
        )
    ]
    for load in loads:
        load.start()

    peers_tm = [at(tm_=(tm + k) % TM) for k in range(1, TM)]
    partner = at(space_=y * 2 + 1 - core)
    y_plus, y_minus = (at(space_=((y + k) % YS) * 2 + core) for k in (1, 3))
    x_plus, x_minus = (at(tm_=zlo * XS + (x + k) % XS) for k in (1, 3))
    peers_dp = [at(dp_=(dp + k) % DP) for k in range(1, DP)]
    barrier = pltpu.get_barrier_semaphore()
    greeted = peers_tm + [partner, y_plus, y_minus] + peers_dp
    for peer in greeted:
        pl.semaphore_signal(barrier, inc=1, device_id=peer, device_id_type=MESH)
    pl.semaphore_wait(barrier, len(greeted))

    def remote(src, dst, sem, device, landed=None):
        return pltpu.make_async_remote_copy(
            src_ref=src,
            dst_ref=dst,
            send_sem=send_sem.at[sem],
            recv_sem=recv_sem.at[sem if landed is None else landed],
            device_id=device,
            device_id_type=MESH,
        )

    def exchange(send, recv, first):
        copies = [
            remote(send.at[(tm + k) % TM], recv.at[tm], first + k, at(tm_=(tm + k) % TM), landed=first + k)
            for k in range(1, TM)
        ]
        own = pltpu.make_async_copy(send.at[tm], recv.at[tm], local_sem.at[7 + first // TM])
        for copy in copies:
            copy.start()
        own.start()

        def receive():
            for k in range(1, TM):
                src = (tm + TM - k) % TM
                remote(send.at[src], recv.at[src], first + k, at(tm_=src)).wait_recv()
            own.wait()

        return copies, receive

    def pack(src, dst):
        for j in range(TM):
            rows = src[OWN * j : OWN * (j + 1), :].astype(F32)
            dst[j, :, :C2] = rows[:16].astype(BF16)
            dst[j, :, C2:] = fold_tail(rows[16:]).astype(BF16)

    def unpack_attn(src, dst):
        for g in range(2):
            rows = [src[f, :, :C2].astype(F32)[8 * g : 8 * g + 8] for f in range(TM)]
            dst[64 * g : 64 * g + 64, :] = jnp.concatenate(rows, axis=0).astype(BF16)
        rows = [open_tail(src[f, :, C2:].astype(F32)) for f in range(TM)]
        dst[128:192, :] = jnp.concatenate(rows, axis=0).astype(BF16)

    prev, nxt = at(tm_=(tm + TM - 1) % TM), at(tm_=(tm + 1) % TM)
    halo_first = remote(frames.at[0, 0], ext.at[FINE + 1], 24, prev)
    halo_last = remote(frames.at[0, FINE - 1], ext.at[0], 25, nxt)
    halo_first.start()
    halo_last.start()

    loads[2].wait()
    pack(go, g_send)

    loads[0].wait()
    loads[1].wait()
    for lo, hi in COLS_FINE:
        n = hi - lo
        pre[:, :, lo:hi] = dot(ext[1:5].reshape(FINE * PIX, C1), wt[C1 : 2 * C1, lo:hi]).reshape(FINE, PIX, n)
        pre[1:4, :, lo:hi] += dot(ext[1:4].reshape(3 * PIX, C1), wt[:C1, lo:hi]).reshape(3, PIX, n)
        pre[0:3, :, lo:hi] += dot(ext[2:5].reshape(3 * PIX, C1), wt[2 * C1 :, lo:hi]).reshape(3, PIX, n)

    halo_first.wait_recv()
    halo_last.wait_recv()
    g_copies, g_receive = exchange(g_send, g_recv, 0)

    def clear_ends(cells):
        @pl.when(tm == 0)
        def _():
            cells[0] = jnp.zeros((PIX, C1), BF16)

        @pl.when(tm == TM - 1)
        def _():
            cells[FINE + 1] = jnp.zeros((PIX, C1), BF16)

    clear_ends(ext)
    for lo, hi in COLS_FINE:
        pre[0, :, lo:hi] += dot(ext[0], wt[:C1, lo:hi])
        pre[3, :, lo:hi] += dot(ext[5], wt[2 * C1 :, lo:hi])
        total = None
        for t in range(FINE):
            act = pre[t, :, lo:hi]
            logistic = 1.0 / (1.0 + jnp.exp(-act))
            skip = (ext[t + 1, :, lo:hi].astype(F32) + act * logistic).astype(BF16).astype(F32)
            total = skip if total is None else total + skip
            pre[t, :, lo:hi] = logistic * (1.0 + act * (1.0 - logistic))
        skipsum[:, lo:hi] = total.astype(BF16)

    loads[3].wait()
    for lo, hi in COLS_COARSE:
        work[:, lo:hi] = 0.25 * dot(skipsum[...], wd[:, lo:hi])
    pack(work, c_send)
    c_copies, c_receive = exchange(c_send, c_recv, 8)

    loads[4].wait()
    loads[5].wait()
    c_receive()
    unpack_attn(c_recv, cb)
    for lo, hi in COLS_COARSE:
        qf[:, lo:hi] = dot(cb[...], wq[:, lo:hi])
        kf[:, lo:hi] = dot(cb[...], wk[:, lo:hi])
    g_receive()
    unpack_attn(g_recv, gb)

    row_i = lax.broadcasted_iota(jnp.int32, (128, 128), 0)
    col_i = lax.broadcasted_iota(jnp.int32, (128, 128), 1)
    ones = ((row_i // DH) == (col_i // DH)).astype(F32).astype(BF16)
    mask = ((row_i[:64] % 8) == (col_i[:64] % 8)).astype(F32)
    left = (lax.broadcasted_iota(jnp.int32, (64, 128), 1) < DH).astype(F32)
    left_b, right_b = left.astype(BF16), (1.0 - left).astype(BF16)

    def heads(rows):
        return jnp.concatenate([rows * left_b, rows * right_b], axis=0)

    def attend(i, carry):
        cols = pl.ds(pl.multiple_of(i * 128, 128), 128)
        q, k = qf[:, cols], kf[:, cols]
        rq = lax.rsqrt(dot((q * q).astype(BF16), ones) * (1.0 / DH) + EPS)
        rk = lax.rsqrt(dot((k * k).astype(BF16), ones) * (1.0 / DH) + EPS)
        qn, kn = q * rq, k * rk
        qb, kb = qn.astype(BF16), kn.astype(BF16)
        bqn, bkn = [], []
        for g in range(3):
            rows = slice(64 * g, 64 * g + 64)
            cg, gg = cb[rows, cols], gb[rows, cols]
            keys = heads(kb[rows])
            raised = jnp.exp(dot_last(qb[rows], keys) * 0.125) * mask
            probs = raised / dot(raised.astype(BF16), ones)
            back_probs = dot_last(gg, heads(cg))
            back_scores = probs * (back_probs - dot((probs * back_probs).astype(BF16), ones))
            probs_b, scores_b = probs.astype(BF16), back_scores.astype(BF16)
            values = dot_first(probs_b, gg)
            back_k = dot_first(scores_b, qb[rows])
            work[rows, cols] = gg.astype(F32) + values[:64] * left + values[64:] * (1.0 - left)
            bkn.append((back_k[:64] * left + back_k[64:] * (1.0 - left)) * 0.125)
            bqn.append(dot(scores_b, keys) * 0.125)
        bqn, bkn = jnp.concatenate(bqn, axis=0), jnp.concatenate(bkn, axis=0)
        bq[:, cols] = (rq * (bqn - qn * (dot((bqn * qn).astype(BF16), ones) * (1.0 / DH)))).astype(BF16)
        bk[:, cols] = (rk * (bkn - kn * (dot((bkn * kn).astype(BF16), ones) * (1.0 / DH)))).astype(BF16)
        return carry

    lax.fori_loop(0, C2 // 128, attend, 0)
    for lo, hi in COLS_COARSE:
        work[:, lo:hi] += dot_last(bq[...], wq[lo:hi, :]) + dot_last(bk[...], wk[lo:hi, :])
    for f in range(TM):
        rows = [work[64 * g + 8 * f : 64 * g + 8 * f + 8, :] for g in range(3)]
        b_send[f, :, :C2] = jnp.concatenate(rows[:2], axis=0).astype(BF16)
        b_send[f, :, C2:] = fold_tail(rows[2]).astype(BF16)
    b_copies, b_receive = exchange(b_send, b_recv, 16)
    b_receive()
    for j in range(0, TM, 2):
        rows = []
        for src in (j, j + 1):
            rows += [b_recv[src, :, :C2].astype(F32), open_tail(b_recv[src, :, C2:].astype(F32))]
        bc[OWN * j : OWN * (j + 2), :] = jnp.concatenate(rows, axis=0).astype(BF16)

    d_sum[C1:, :] = jnp.zeros((8, C2), F32)

    def down(i, carry):
        cols = pl.ds(pl.multiple_of(i * 128, 128), 128)
        d_sum[cols, :] = dot_first(skipsum[:, cols], bc[...])
        return carry

    lax.fori_loop(0, C1 // 128, down, 0)

    def down_unit(part_y, part_core, part_dp):
        odd = part_dp % 2 * 4
        start = pl.multiple_of(160 * part_y + 80 * part_core + (20 * part_dp - odd), 8)
        rows = d_sum[pl.ds(start, 32 if odd else 24), :][odd : odd + 24]
        return jnp.concatenate([rows[:, :C1], rows[:, C1:], jnp.zeros((16, C1), F32)], axis=0).reshape(4, 16, C1)

    def time_unit(part_y, part_core, part_dp):
        odd = part_dp % 2 * 4
        start = pl.multiple_of(480 * part_y + 240 * part_core + (60 * part_dp - odd), 8)
        return t_sum[pl.ds(start, 72 if odd else 64), :][odd : odd + 64]

    def pack_down(part_y, carry):
        for h in range(DP):
            cs_x[:, part_y, h] = down_unit(part_y, 1 - core, h).astype(BF16)
        return carry

    lax.fori_loop(0, YS, pack_down, 0)
    swap_x = remote(cs_x, p_x, 26, partner)
    swap_x.start()

    loads[6].wait()
    for lo, hi in COLS_FINE:
        spread[:, lo:hi] = 0.25 * dot_last(bc[...], wd[lo:hi, :])
        for t in range(FINE):
            back = gs[t, :, lo:hi].astype(F32) + spread[:, lo:hi]
            bpe[t + 1, :, lo:hi] = (back * pre[t, :, lo:hi]).astype(BF16)
    back_first = remote(bpe.at[1], bpe.at[FINE + 1], 28, prev)
    back_last = remote(bpe.at[FINE], bpe.at[0], 29, nxt)
    back_first.start()
    back_last.start()

    swap_x.wait_recv()

    def add_down(part_y, carry):
        for h in range(DP):
            p_x[:, part_y, h] = (p_x[:, part_y, h].astype(F32) + down_unit(part_y, core, h)).astype(BF16)
        return carry

    lax.fori_loop(0, YS, add_down, 0)
    ring_x = Ring(remote, p_x, (x_ra, x_rb, x_fp, x_fm), x, x_plus, x_minus, 30)
    ring_x.start()

    t_sum[3 * C1 :, :] = jnp.zeros((8, C1), F32)
    for k in range(3):

        def time_block(i, carry, k=k):
            cols = pl.ds(pl.multiple_of(i * 128, 128), 128)
            block = ext[k : k + FINE, :, cols].reshape(FINE * PIX, 128)
            start = pl.multiple_of(k * C1 + i * 128, 128)
            t_sum[pl.ds(start, 128), :] = dot_first(block, bpe[1 : FINE + 1].reshape(FINE * PIX, C1))
            return carry

        lax.fori_loop(0, C1 // 128, time_block, 0)

    def pack_time(part_y, carry):
        for h in range(DP):
            cs_y[part_y, h] = time_unit(part_y, 1 - core, h).astype(BF16)
        return carry

    lax.fori_loop(0, YS, pack_time, 0)
    swap_y = remote(cs_y, p_y, 27, partner)
    swap_y.start()
    ring_x.middle()
    swap_y.wait_recv()

    def add_time(part_y, carry):
        for h in range(DP):
            p_y[part_y, h] = (p_y[part_y, h].astype(F32) + time_unit(part_y, core, h)).astype(BF16)
        return carry

    lax.fori_loop(0, YS, add_time, 0)
    ring_y = Ring(remote, p_y, (y_ra, y_rb, y_fp, y_fm), y, y_plus, y_minus, 36)
    ring_y.start()

    back_first.wait_recv()
    back_last.wait_recv()
    clear_ends(bpe)
    for lo, hi in COLS_FINE:
        n = hi - lo
        for t in range(0, FINE, 2):
            rows = [bpe[t + k : t + k + 2].reshape(2 * PIX, C1) for k in range(3)]
            acc = dot_last(rows[2], wt[lo:hi, :])
            acc += dot_last(rows[1], wt[C1 + lo : C1 + hi, :])
            acc += dot_last(rows[0], wt[2 * C1 + lo : 2 * C1 + hi, :])
            acc = acc.reshape(2, PIX, n) + gs[t : t + 2, :, lo:hi].astype(F32) + spread[:, lo:hi]
            gs[t : t + 2, :, lo:hi] = acc.astype(BF16)
    store = pltpu.make_async_copy(gs, ig_out.at[0], local_sem.at[10])
    store.start()

    ring_x.arrived()
    for part_y in range(YS):
        p2_x[part_y] = ring_x.total(part_y).astype(BF16)
    ring2_x = Ring(remote, p2_x, (x2_ra, x2_rb, x2_fp, x2_fm), y, y_plus, y_minus, 42)
    ring2_x.start()
    ring_y.middle()
    ring2_x.middle()
    ring_y.arrived()
    for h in range(DP):
        p2_y[:, h] = ring_y.total(h).astype(BF16).reshape(XS, 16, C1)
    ring2_y = Ring(remote, p2_y, (y2_ra, y2_rb, y2_fp, y2_fm), x, x_plus, x_minus, 48)
    ring2_y.start()
    ring2_y.middle()
    ring2_x.arrived()
    for h in range(DP):
        z_buf[1, h] = ring2_x.total(h).astype(BF16)
    ring2_y.arrived()
    for h in range(DP):
        z_buf[0, h] = ring2_y.total(h).astype(BF16)

    swap_z = remote(z_buf.at[1 - zlo], z_recv, 54, at(tm_=(1 - zlo) * XS + x))
    swap_z.start()
    swap_z.wait_recv()
    w_buf[...] = (z_buf[zlo].astype(F32) + z_recv[...].astype(F32)).astype(BF16)
    dp_copies = [remote(w_buf.at[(dp + k) % DP], w_recv.at[k - 1], 54 + k, peers_dp[k - 1]) for k in range(1, DP)]
    for copy in dp_copies:
        copy.start()
    total = w_buf[dp].astype(F32)
    for k in range(1, DP):
        dp_copies[k - 1].wait_recv()
        total += w_recv[k - 1].astype(F32)
    final[tm] = total.astype(BF16)
    last_copies = [remote(final.at[tm], final.at[tm], 57 + k, peers_tm[k - 1]) for k in range(1, TM)]
    for copy in last_copies:
        copy.start()
    for k in range(1, TM):
        src = (tm + TM - k) % TM
        remote(final.at[src], final.at[src], 57 + k, at(tm_=src)).wait_recv()
    scale = 1.0 / math.sqrt(ROWS_ALL)
    time_out[...] = (final[0:4].astype(F32) * scale).reshape(64, C1)[:60]
    rows = (final[4:7].astype(F32) * (0.25 * scale)).reshape(48, C1)
    down_out[:, :C1] = rows[:20]
    down_out[:, C1:] = rows[24:44]

    for copy in [halo_first, halo_last, back_first, back_last, swap_x, swap_y, swap_z]:
        copy.wait_send()
    for copy in g_copies + c_copies + b_copies + dp_copies + last_copies:
        copy.wait_send()
    for ring in (ring_x, ring_y, ring2_x, ring2_y):
        ring.finish()
    store.wait()


def shards(*args):
    v = pltpu.VMEM
    scratch = [
        v((FINE + 2, PIX, C1), BF16), v((3 * C1, C1), BF16), v((C1, C2), BF16), v((C2, C2), BF16), v((C2, C2), BF16),
        v((FINE, PIX, C1), BF16), v((PIX, C2), BF16), v((FINE, PIX, C1), F32), v((PIX, C1), BF16),
        v((PIX, C2), F32), v((PIX, C2), F32), v((PIX, C2), F32),
        v((PIX, C2), BF16), v((PIX, C2), BF16), v((PIX, C2), BF16), v((PIX, C2), BF16),
        *[v((TM, 16, C2 + C1), BF16)] * 6,
        v((PIX, C2), BF16), v((PIX, C1), F32), v((FINE + 2, PIX, C1), BF16),
        v((3 * C1 + 8, C1), F32), v((C1 + 8, C2), F32),
        v((YS, DP, 64, C1), BF16), v((XS, YS, DP, 16, C1), BF16),
        v((YS, DP, 64, C1), BF16), v((XS, YS, DP, 16, C1), BF16),
        *[v((2, 64, C1), BF16)] * 2, *[v((4, 64, C1), BF16)] * 2,
        *[v((2, DP, 16, C1), BF16)] * 2, *[v((4, DP, 16, C1), BF16)] * 2,
        v((XS, DP, 16, C1), BF16), v((YS, DP, 16, C1), BF16),
        *[v((2, 16, C1), BF16)] * 2, *[v((4, 16, C1), BF16)] * 2,
        *[v((2, 16, C1), BF16)] * 2, *[v((4, 16, C1), BF16)] * 2,
        v((2, DP, 16, C1), BF16), v((DP, 16, C1), BF16), v((DP, 16, C1), BF16), v((DP - 1, 16, C1), BF16),
        v((TM, 16, C1), BF16),
        pltpu.SemaphoreType.DMA((11,)), pltpu.SemaphoreType.DMA((65,)), pltpu.SemaphoreType.DMA((65,)),
    ]
    return pl.pallas_call(
        kernel,
        out_shape=(
            jax.ShapeDtypeStruct((1, FINE, PIX, C1), BF16),
            jax.ShapeDtypeStruct((60, C1), F32),
            jax.ShapeDtypeStruct((20, C2), F32),
        ),
        in_specs=[pl.BlockSpec(memory_space=pl.ANY)] * 7,
        out_specs=(
            pl.BlockSpec(memory_space=pl.ANY),
            pl.BlockSpec(memory_space=pltpu.VMEM),
            pl.BlockSpec(memory_space=pltpu.VMEM),
        ),
        scratch_shapes=scratch,
        compiler_params=pltpu.CompilerParams(
            collective_id=0, has_side_effects=True, vmem_limit_bytes=62 * 1024 * 1024
        ),
        cost_estimate=pl.CostEstimate(flops=9 * 10**9, bytes_accessed=16 * 10**6, transcendentals=10**6),
    )(*args)


def solution(mesh):
    fine, whole = P("dp", "tm", "space", None), P()
    rows = P(("space", "dp"), None)
    return jax.shard_map(
        shards,
        mesh=mesh,
        in_specs=(fine, whole, whole, whole, whole, fine, fine),
        out_specs=(fine, rows, rows),
        check_vma=False,
    )
```

time: 568 us -> 116 us (0.20)
  blocking collectives: 207 us -> 0 us
  Pallas kernels: 0 us -> 109 us
  local copies, waits for them, and re-layouts: 91.6 us -> 5.38 us
  waiting for transfers between devices: 73.2 us -> 0 us
  starting transfers between devices: 69.8 us -> 0 us
  matrix products: 65.9 us -> 0 us
  other arithmetic: 39.2 us -> 0 us
  between operations: 15.4 us -> 0.64 us
    unnamed x1 -> x0, blocking collectives: 207 us -> none
    pallas_call x0 -> x1, Pallas kernels: none -> 109 us  [shards(): pl.pallas_call(kernel, out_shape=(jax.ShapeDtypeStruct((1, FINE, PIX, C1)...]
    psum x1 -> x0, waiting for transfers between devices: 69.2 us -> none  [shards(): time_part, down_part = lax.psum((time_part, down_part), 'tm')]
    dot_general x17 -> x0, matrix products: 65.9 us -> none  [the longest x6 14.9 us: contract_last(): lax.dot_general(left_mat, right_mat, (((1,), (1,)), ((), ())), preferred_...]
    unnamed x75 -> x3, local copies, waits for them, and re-layouts: 39.2 us -> 5.38 us
    unnamed x8 -> x0, starting transfers between devices: 32.9 us -> none
    reshape x7 -> x0, local copies, waits for them, and re-layouts: 20.3 us -> none  [the longest x2 6.34 us: coarse_backward(): jnp.dot(coarse_rows, w_key, preferred_element_type=jnp.float32)]
    all_to_all x3 -> x0, starting transfers between devices: 18.8 us -> none  [the longest x1 7.17 us: shards(): lax.all_to_all(grad_out, 'tm', split_axis=2, concat_axis=1, tiled=True)]
  transfers between devices with their start and end apart: 16 -> 0, of which waited for: 2 -> 0; matrix products, arithmetic and copies ran while one was open for 13% -> 0% of each run, Pallas kernels for 0% -> 0%
where the time goes in v1:
time: 116 us; the launch traced here: 115 us
  Pallas kernels  109 us (94%)
  local copies, waits for them, and re-layouts  5.38 us (5%)
    pallas_call x1, Pallas kernels, shards(): pl.pallas_call(kernel, out_shape=(jax.ShapeDtypeStruct((1, FINE, PIX, C1)...  109 us
    unnamed x3, local copies, waits for them, and re-layouts  5.38 us

profile of v1, /device:TPU:2, one launch (start us, length us, event | category | flops | bytes accessed | tf_op | source)
XLA Modules:
  0.0 115.4 jit_solution(359792450604401196)
XLA Ops:
  0.6 109.4 %shard_map.94 = (bf16[1,4,192,640]{3,2,1,0:T(8,128)(2,1)}, f32[60,640]{1,0:T(8,128)}, f32[20,1280]{1,0:T(8,128)}) custom-call(bf16[1,4,192,640]{3,2,1,0:T(8,128)(2,1)} %frames.1, bf16[1920,640]{1,0:T(8,128)(2,1)} %w_time.1, bf16[640,1280]{1,0:T(8,128)(2,1)} %w_down.1, bf16[1280,1280]{1,0:T(8,128)(2,1)} %w_query.1, bf16[1280,1280]{1,0:T(8,128)(2,1)} %w_key.1, ...), custom_call_target="tpu_custom_call" | custom-call | flops 8999999488 | bytes 16000000 | tf_op jit(solution)/shard_map/pallas_call | solution.py:454
  110.0 2.2 %copy.13 = bf16[1,4,192,640]{3,2,1,0:T(8,128)(2,1)} copy(bf16[1,4,192,640]{3,2,1,0:T(8,128)(2,1)} %get-tuple-element.6) | data formatting | bytes 1966080
  112.2 1.6 %copy.14 = f32[60,640]{1,0:T(8,128)} copy(f32[60,640]{1,0:T(8,128)} %get-tuple-element.7) | data formatting | bytes 307200
  113.8 1.6 %copy.15 = f32[20,1280]{1,0:T(8,128)} copy(f32[20,1280]{1,0:T(8,128)} %get-tuple-element.8) | data formatting | bytes 204800

commit v2 on v1

v2 whole, which is shorter than its diff:
```python
import math

import jax
import jax.numpy as jnp
from jax import lax
from jax.experimental import pallas as pl
from jax.experimental.pallas import tpu as pltpu
from jax.sharding import PartitionSpec as P

C1, C2, DH = 640, 1280, 64
TM, YS, XS, DP = 8, 4, 4, 4
FINE, PIX = 4, 192
ROWS_ALL = 4 * 32 * 1536
EPS = 1e-06
MESH = pl.DeviceIdType.MESH
F32, BF16 = jnp.float32, jnp.bfloat16
COLS_FINE = ((0, 256), (256, 512), (512, 640))
COLS_COARSE = tuple((n, n + 256) for n in range(0, C2, 256))
CHUNKS, WIDE = 3, 64
DC = 512
TILES = 5


def dot(left, right):
    return jnp.dot(left, right, preferred_element_type=F32)


def dot_last(left, right):
    return lax.dot_general(left, right, (((1,), (1,)), ((), ())), preferred_element_type=F32)


def dot_first(left, right):
    return lax.dot_general(left, right, (((0,), (0,)), ((), ())), preferred_element_type=F32)


def fold_tail(tail):
    return jnp.concatenate([tail[:, :C1], tail[:, C1:]], axis=0)


def open_tail(tail):
    return jnp.concatenate([tail[:8], tail[8:]], axis=1)


class Ring:
    def __init__(self, remote, parts, bufs, pos, plus, minus, first):
        self.parts, self.pos = parts, pos
        self.ra, self.rb, self.fp, self.fm = bufs
        lo, hi = pl.ds(0, 2), pl.ds(2, 2)
        self.ahead, self.behind, self.far = (pos + 1) % 4, (pos + 3) % 4, (pos + 2) % 4
        self.copies = [
            remote(parts.at[self.far, lo], self.ra, first, plus),
            remote(parts.at[self.far, hi], self.rb, first + 1, minus),
            remote(parts.at[self.ahead, hi], self.fp.at[hi], first + 2, plus),
            remote(parts.at[self.behind, lo], self.fm.at[lo], first + 3, minus),
            remote(parts.at[self.ahead, lo], self.fp.at[lo], first + 4, plus),
            remote(parts.at[self.behind, hi], self.fm.at[hi], first + 5, minus),
        ]

    def start(self):
        for copy in self.copies[:4]:
            copy.start()

    def middle(self):
        parts = self.parts
        self.copies[0].wait_recv()
        parts[self.ahead, 0:2] = (parts[self.ahead, 0:2].astype(F32) + self.ra[...].astype(F32)).astype(BF16)
        self.copies[4].start()
        self.copies[1].wait_recv()
        parts[self.behind, 2:4] = (parts[self.behind, 2:4].astype(F32) + self.rb[...].astype(F32)).astype(BF16)
        self.copies[5].start()

    def arrived(self):
        for copy in self.copies[2:]:
            copy.wait_recv()

    def total(self, i):
        return self.parts[self.pos, i].astype(F32) + self.fp[i].astype(F32) + self.fm[i].astype(F32)

    def finish(self):
        for copy in self.copies:
            copy.wait_send()


def attend(tiles, qf, kf, cb, gb, work, bq, bk):
    row_i = lax.broadcasted_iota(jnp.int32, (128, 128), 0)
    col_i = lax.broadcasted_iota(jnp.int32, (128, 128), 1)
    ones = ((row_i // DH) == (col_i // DH)).astype(F32).astype(BF16)
    mask = ((row_i[:WIDE] % 8) == (col_i[:WIDE] % 8)).astype(F32)
    left = (lax.broadcasted_iota(jnp.int32, (WIDE, 128), 1) < DH).astype(F32)
    left_b, right_b = left.astype(BF16), (1.0 - left).astype(BF16)
    count = len(tiles)
    units = [(i, slice(WIDE * g, WIDE * g + WIDE)) for i in range(count) for g in range(CHUNKS)]
    index = range(len(units))

    def heads(rows):
        return jnp.concatenate([rows * left_b, rows * right_b], axis=0)

    def fold(both):
        return jnp.where(left > 0.5, both[:WIDE], both[WIDE:])

    def head_sums(terms):
        sums = dot(jnp.concatenate([term.astype(BF16) for term in terms], axis=0), ones)
        rows = terms[0].shape[0]
        return [sums[rows * i : rows * i + rows] for i in range(len(terms))]

    q, k = [qf[:, c] for c in tiles], [kf[:, c] for c in tiles]
    factors = [lax.rsqrt(total * (1.0 / DH) + EPS) for total in head_sums([v * v for v in q + k])]
    rq, rk = factors[:count], factors[count:]
    qb = [(q[i] * rq[i]).astype(BF16) for i in range(count)]
    kb = [(k[i] * rk[i]).astype(BF16) for i in range(count)]
    queries = [qb[i][rows] for i, rows in units]
    keys = [heads(kb[i][rows]) for i, rows in units]
    raised = [jnp.exp(dot_last(queries[n], keys[n]) * 0.125) * mask for n in index]
    upstream = [gb[rows, tiles[i]] for i, rows in units]
    back_probs = [dot_last(upstream[n], heads(cb[rows, tiles[i]])) for n, (i, rows) in enumerate(units)]
    probs = [over / under for over, under in zip(raised, head_sums(raised))]
    means = head_sums([p * b for p, b in zip(probs, back_probs)])
    scores = [(p * (b - m)).astype(BF16) for p, b, m in zip(probs, back_probs, means)]
    for n, (i, rows) in enumerate(units):
        values = fold(dot_first(probs[n].astype(BF16), upstream[n]))
        work[rows, tiles[i]] = upstream[n].astype(F32) + values
    back_q = [dot(scores[n], keys[n]) * 0.125 for n in index]
    back_k = [fold(dot_first(scores[n], queries[n])) * 0.125 for n in index]
    qn = [rows.astype(F32) for rows in queries]
    kn = [kb[i][rows].astype(F32) for i, rows in units]
    mean_q = head_sums([b * v for b, v in zip(back_q, qn)])
    mean_k = head_sums([b * v for b, v in zip(back_k, kn)])
    for n, (i, rows) in enumerate(units):
        bq[rows, tiles[i]] = (rq[i][rows] * (back_q[n] - qn[n] * (mean_q[n] * (1.0 / DH)))).astype(BF16)
        bk[rows, tiles[i]] = (rk[i][rows] * (back_k[n] - kn[n] * (mean_k[n] * (1.0 / DH)))).astype(BF16)


def kernel(
    frames, w_time, w_down, w_query, w_key, grad_skip, grad_out,
    ig_out, sums_out,
    ext, wt, wd, wq, wk, gs, go, pre, skipsum, work, qf, kf, cb, gb, bq, bk,
    g_send, g_recv, c_send, c_recv, b_send, b_recv, bc, spread, bpe,
    t_sum, d_sum, cs_y, cs_x, p_y, p_x, y_ra, y_rb, y_fp, y_fm, x_ra, x_rb, x_fp, x_fm,
    p2_y, p2_x, y2_ra, y2_rb, y2_fp, y2_fm, x2_ra, x2_rb, x2_fp, x2_fm,
    z_buf, z_recv, final,
    local_sem, send_sem, recv_sem,
):
    tm, space, dp = lax.axis_index("tm"), lax.axis_index("space"), lax.axis_index("dp")
    core, y, zlo, x = space % 2, space // 2, tm // XS, tm % XS

    def at(tm_=None, space_=None, dp_=None):
        return {
            "tm": tm if tm_ is None else tm_,
            "space": space if space_ is None else space_,
            "dp": dp if dp_ is None else dp_,
        }

    loads = [
        pltpu.make_async_copy(src, dst, local_sem.at[i])
        for i, (src, dst) in enumerate(
            (
                (frames.at[0], ext.at[pl.ds(1, FINE)]),
                (w_time, wt),
                (w_down, wd),
                (grad_out.at[0, 0], go),
                (w_query, wq),
                (w_key, wk),
                (grad_skip.at[0], gs),
            )
        )
    ]
    for load in loads:
        load.start()

    peers_tm = [at(tm_=(tm + k) % TM) for k in range(1, TM)]
    partner = at(space_=y * 2 + 1 - core)
    y_plus, y_minus = (at(space_=((y + k) % YS) * 2 + core) for k in (1, 3))
    x_plus, x_minus = (at(tm_=zlo * XS + (x + k) % XS) for k in (1, 3))
    zpos = dp * 2 + zlo
    on_z = [(zpos + k) % 8 for k in range(1, 8)]
    peers_z = [at(tm_=z % 2 * XS + x, dp_=z // 2) for z in on_z]
    barrier = pltpu.get_barrier_semaphore()
    other_z = [at(tm_=tm_, dp_=(dp + k) % DP) for k in range(1, DP) for tm_ in (x, XS + x)]
    greeted = peers_tm + [partner, y_plus, y_minus] + other_z
    for peer in greeted:
        pl.semaphore_signal(barrier, inc=1, device_id=peer, device_id_type=MESH)
    pl.semaphore_wait(barrier, len(greeted))

    def remote(src, dst, sem, device, landed=None):
        return pltpu.make_async_remote_copy(
            src_ref=src,
            dst_ref=dst,
            send_sem=send_sem.at[sem],
            recv_sem=recv_sem.at[sem if landed is None else landed],
            device_id=device,
            device_id_type=MESH,
        )

    def exchange(send, recv, c, first):
        copies = [
            remote(send.at[c, (tm + k) % TM], recv.at[c, tm], first + k, at(tm_=(tm + k) % TM)) for k in range(1, TM)
        ]
        own = pltpu.make_async_copy(send.at[c, tm], recv.at[c, tm], local_sem.at[7 + first // TM])
        for copy in copies:
            copy.start()
        own.start()

        def receive():
            for k in range(1, TM):
                src = (tm + TM - k) % TM
                remote(send.at[c, src], recv.at[c, src], first + k, at(tm_=src)).wait_recv()
            own.wait()

        sent.extend(copies)
        return receive

    sent = []

    def send(copy):
        copy.start()
        sent.append(copy)
        return copy

    def pack(src, dst, c):
        rows = src[c * WIDE : (c + 1) * WIDE, :].astype(F32)
        for f in range(TM):
            dst[c, f] = fold_tail(rows[8 * f : 8 * f + 8]).astype(BF16)

    def unpack(src, dst, c):
        rows = [open_tail(src[c, f].astype(F32)) for f in range(TM)]
        dst[c * WIDE : (c + 1) * WIDE, :] = jnp.concatenate(rows, axis=0).astype(BF16)

    prev, nxt = at(tm_=(tm + TM - 1) % TM), at(tm_=(tm + 1) % TM)
    halos = []
    for c in range(CHUNKS):
        rows = pl.ds(c * WIDE, WIDE)
        first = send(remote(frames.at[0, 0, rows], ext.at[FINE + 1, rows], 72 + 2 * c, prev))
        last = send(remote(frames.at[0, FINE - 1, rows], ext.at[0, rows], 73 + 2 * c, nxt))
        halos.append((first, last))

    loads[0].wait()
    loads[1].wait()
    for lo, hi in COLS_FINE:
        n = hi - lo
        pre[:, :, lo:hi] = dot(ext[1:5].reshape(FINE * PIX, C1), wt[C1 : 2 * C1, lo:hi]).reshape(FINE, PIX, n)
        pre[1:4, :, lo:hi] += dot(ext[1:4].reshape(3 * PIX, C1), wt[:C1, lo:hi]).reshape(3, PIX, n)
        pre[0:3, :, lo:hi] += dot(ext[2:5].reshape(3 * PIX, C1), wt[2 * C1 :, lo:hi]).reshape(3, PIX, n)
    loads[3].wait()
    for c in range(CHUNKS):
        pack(go, g_send, c)

    loads[2].wait()
    c_receive, g_receive = [], []
    for c in range(CHUNKS):
        rows = slice(c * WIDE, (c + 1) * WIDE)
        for copy in halos[c]:
            copy.wait_recv()

        @pl.when(tm == 0)
        def _():
            ext[0, rows] = jnp.zeros((WIDE, C1), BF16)

        @pl.when(tm == TM - 1)
        def _():
            ext[FINE + 1, rows] = jnp.zeros((WIDE, C1), BF16)

        for lo, hi in COLS_FINE:
            pre[0, rows, lo:hi] += dot(ext[0, rows], wt[:C1, lo:hi])
            pre[3, rows, lo:hi] += dot(ext[5, rows], wt[2 * C1 :, lo:hi])
            total = None
            for t in range(FINE):
                act = pre[t, rows, lo:hi]
                logistic = 1.0 / (1.0 + jnp.exp(-act))
                skip = (ext[t + 1, rows, lo:hi].astype(F32) + act * logistic).astype(BF16).astype(F32)
                total = skip if total is None else total + skip
                pre[t, rows, lo:hi] = logistic * (1.0 + act * (1.0 - logistic))
            skipsum[rows, lo:hi] = total.astype(BF16)
        for lo, hi in COLS_COARSE:
            work[rows, lo:hi] = 0.25 * dot(skipsum[rows, :], wd[:, lo:hi])
        pack(work, c_send, c)
        c_receive.append(exchange(c_send, c_recv, c, 8 * c))
    for c in range(CHUNKS):
        g_receive.append(exchange(g_send, g_recv, c, 24 + 8 * c))

    loads[4].wait()
    loads[5].wait()
    for c in range(CHUNKS):
        c_receive[c]()
        unpack(c_recv, cb, c)
    for lo, hi in COLS_COARSE:
        qf[:, lo:hi] = dot(cb[...], wq[:, lo:hi])
        kf[:, lo:hi] = dot(cb[...], wk[:, lo:hi])
    for c in range(CHUNKS):
        g_receive[c]()
        unpack(g_recv, gb, c)

    def attend_some(i, carry):
        tiles = [pl.ds(pl.multiple_of((i * TILES + u) * 128, 128), 128) for u in range(TILES)]
        attend(tiles, qf, kf, cb, gb, work, bq, bk)
        return carry

    lax.fori_loop(0, C2 // 128 // TILES, attend_some, 0)
    for lo, hi in COLS_COARSE:
        work[:, lo:hi] += dot_last(bq[...], wq[lo:hi, :]) + dot_last(bk[...], wk[lo:hi, :])
    b_receive = []
    for c in range(CHUNKS):
        pack(work, b_send, c)
        b_receive.append(exchange(b_send, b_recv, c, 48 + 8 * c))
    for c in range(CHUNKS):
        b_receive[c]()
        unpack(b_recv, bc, c)

    loads[6].wait()
    for lo, hi in COLS_FINE:
        spread[:, lo:hi] = 0.25 * dot_last(bc[...], wd[lo:hi, :])
        for t in range(FINE):
            back = gs[t, :, lo:hi].astype(F32) + spread[:, lo:hi]
            bpe[t + 1, :, lo:hi] = (back * pre[t, :, lo:hi]).astype(BF16)
    back_first = send(remote(bpe.at[1], bpe.at[FINE + 1], 78, prev))
    back_last = send(remote(bpe.at[FINE], bpe.at[0], 79, nxt))

    def time_unit(part_y, part_core, part_dp):
        start = pl.multiple_of(480 * part_y + 240 * part_core + 60 * part_dp // 8 * 8, 8)
        return t_sum[pl.ds(start, 64), :]

    def down_unit(part_y, part_core, part_dp):
        start = pl.multiple_of(160 * part_y + 80 * part_core + 20 * part_dp // 8 * 8, 8)
        rows = d_sum[pl.ds(start, 24), :]
        return jnp.concatenate([rows[:16], fold_tail(rows[16:]), jnp.zeros((16, 128), F32)], axis=1)

    swap_y = []
    for part_y in range(YS):

        def time_block(i, carry):
            cols = pl.ds(pl.multiple_of(i % 5 * 128, 128), 128)
            block = ext[pl.ds(i // 5, FINE), :, cols].reshape(FINE * PIX, 128)
            start = pl.multiple_of(i * 128, 128)
            t_sum[pl.ds(start, 128), :] = dot_first(block, bpe[1 : FINE + 1].reshape(FINE * PIX, C1))
            return carry

        lax.fori_loop(4 * part_y, min(4 * part_y + 4, 15), time_block, 0)
        for h in range(DP):
            cs_y[part_y, h] = time_unit(part_y, 1 - core, h).astype(BF16)
        swap_y.append(send(remote(cs_y.at[part_y], p_y.at[part_y], 80 + part_y, partner)))

    def down(i, carry):
        cols = pl.ds(pl.multiple_of(i * 128, 128), 128)
        d_sum[cols, :] = dot_first(skipsum[:, cols], bc[...])
        return carry

    lax.fori_loop(0, C1 // 128, down, 0)

    def pack_down(part_y, carry):
        for h in range(DP):
            unit = down_unit(part_y, 1 - core, h).astype(BF16)
            for part_x in range(XS):
                cs_x[part_x, part_y, h] = unit[:, DC * part_x : DC * part_x + DC]
        return carry

    lax.fori_loop(0, YS, pack_down, 0)
    swap_x = send(remote(cs_x, p_x, 84, partner))

    ring_y = Ring(remote, p_y, (y_ra, y_rb, y_fp, y_fm), y, y_plus, y_minus, 86)
    for part_y, copies in (
        (ring_y.far, ring_y.copies[:2]),
        (ring_y.ahead, ring_y.copies[2:3]),
        (ring_y.behind, ring_y.copies[3:4]),
        (y, []),
    ):
        remote(cs_y.at[part_y], p_y.at[part_y], 80 + part_y, partner).wait_recv()
        for h in range(DP):
            p_y[part_y, h] = (p_y[part_y, h].astype(F32) + time_unit(part_y, core, h)).astype(BF16)
        for copy in copies:
            copy.start()

    swap_x.wait_recv()

    def add_down(part_y, carry):
        for h in range(DP):
            unit = down_unit(part_y, core, h)
            for part_x in range(XS):
                more = unit[:, DC * part_x : DC * part_x + DC]
                p_x[part_x, part_y, h] = (p_x[part_x, part_y, h].astype(F32) + more).astype(BF16)
        return carry

    lax.fori_loop(0, YS, add_down, 0)
    ring_x = Ring(remote, p_x, (x_ra, x_rb, x_fp, x_fm), x, x_plus, x_minus, 92)
    ring_x.start()

    back_first.wait_recv()
    back_last.wait_recv()

    @pl.when(tm == 0)
    def _():
        bpe[0] = jnp.zeros((PIX, C1), BF16)

    @pl.when(tm == TM - 1)
    def _():
        bpe[FINE + 1] = jnp.zeros((PIX, C1), BF16)

    def input_grad(lo, hi):
        for t in range(0, FINE, 2):
            rows = [bpe[t + k : t + k + 2].reshape(2 * PIX, C1) for k in range(3)]
            acc = dot_last(rows[2], wt[lo:hi, :])
            acc += dot_last(rows[1], wt[C1 + lo : C1 + hi, :])
            acc += dot_last(rows[0], wt[2 * C1 + lo : 2 * C1 + hi, :])
            acc = acc.reshape(2, PIX, hi - lo) + gs[t : t + 2, :, lo:hi].astype(F32) + spread[:, lo:hi]
            gs[t : t + 2, :, lo:hi] = acc.astype(BF16)

    input_grad(*COLS_FINE[0])
    ring_y.middle()
    input_grad(*COLS_FINE[1])
    ring_x.middle()
    input_grad(*COLS_FINE[2])
    store = pltpu.make_async_copy(gs, ig_out.at[0], local_sem.at[16])
    store.start()

    ring_y.arrived()
    for h in range(DP):
        p2_y[:, h] = ring_y.total(h).astype(BF16).reshape(XS, 16, C1)
    ring2_y = Ring(remote, p2_y, (y2_ra, y2_rb, y2_fp, y2_fm), x, x_plus, x_minus, 98)
    ring2_y.start()
    ring_x.arrived()
    for part_y in range(YS):
        p2_x[part_y] = ring_x.total(part_y).astype(BF16)
    ring2_x = Ring(remote, p2_x, (x2_ra, x2_rb, x2_fp, x2_fm), y, y_plus, y_minus, 104)
    ring2_x.start()
    ring2_y.middle()
    ring2_x.middle()
    ring2_y.arrived()
    for h in range(DP):
        z_buf[0, h] = ring2_y.total(h).astype(BF16)
    ring2_x.arrived()
    for h in range(DP):
        z_buf[1, h, :, :DC] = ring2_x.total(h).astype(BF16)
        z_buf[1, h, :, DC:] = jnp.zeros((16, C1 - DC), BF16)

    z_copies = [
        send(remote(z_buf.at[z % 2, z // 2], z_recv.at[k], 110 + k, peers_z[k])) for k, z in enumerate(on_z)
    ]
    total = z_buf[zlo, dp].astype(F32)
    for k in range(7):
        z_copies[k].wait_recv()
        total += z_recv[k].astype(F32)
    final[tm] = total.astype(BF16)
    for k in range(1, TM):
        send(remote(final.at[tm], final.at[tm], 117 + k, peers_tm[k - 1]))
    for k in range(1, TM):
        src = (tm + TM - k) % TM
        remote(final.at[src], final.at[src], 117 + k, at(tm_=src)).wait_recv()
    sums_out[...] = final[...]

    for copy in sent:
        copy.wait_send()
    for ring in (ring_x, ring_y, ring2_x, ring2_y):
        ring.finish()
    store.wait()


def finish(ig, sums, ig_out, time_out, down_out, sem):
    copy = pltpu.make_async_copy(ig, ig_out, sem)
    copy.start()
    odd = lax.axis_index("dp") % 2 == 1
    scale = 1.0 / math.sqrt(ROWS_ALL)
    rows = sums[:XS].astype(F32).reshape(64, C1) * scale
    time_out[...] = jnp.where(odd, rows[4:64], rows[:60])
    wide = jnp.concatenate([sums[XS + part_x, :, :DC] for part_x in range(XS)], axis=1).astype(F32) * (0.25 * scale)
    rows = jnp.concatenate([wide[:, :C2], open_tail(wide[:, C2 : C2 + C1])], axis=0)
    down_out[...] = jnp.where(odd, rows[4:24], rows[:20])
    copy.wait()


def shards(*args):
    v, hbm = pltpu.VMEM, pl.BlockSpec(memory_space=pl.ANY)
    vmem = pl.BlockSpec(memory_space=pltpu.VMEM)
    scratch = [
        v((FINE + 2, PIX, C1), BF16), v((3 * C1, C1), BF16), v((C1, C2), BF16), v((C2, C2), BF16), v((C2, C2), BF16),
        v((FINE, PIX, C1), BF16), v((PIX, C2), BF16), v((FINE, PIX, C1), F32), v((PIX, C1), BF16),
        v((PIX, C2), F32), v((PIX, C2), F32), v((PIX, C2), F32),
        v((PIX, C2), BF16), v((PIX, C2), BF16), v((PIX, C2), BF16), v((PIX, C2), BF16),
        *[v((CHUNKS, TM, 16, C1), BF16)] * 6,
        v((PIX, C2), BF16), v((PIX, C1), F32), v((FINE + 2, PIX, C1), BF16),
        v((3 * C1, C1), F32), v((C1, C2), F32),
        v((YS, DP, 64, C1), BF16), v((XS, YS, DP, 16, DC), BF16),
        v((YS, DP, 64, C1), BF16), v((XS, YS, DP, 16, DC), BF16),
        *[v((2, 64, C1), BF16)] * 2, *[v((4, 64, C1), BF16)] * 2,
        *[v((2, DP, 16, DC), BF16)] * 2, *[v((4, DP, 16, DC), BF16)] * 2,
        v((XS, DP, 16, C1), BF16), v((YS, DP, 16, DC), BF16),
        *[v((2, 16, C1), BF16)] * 2, *[v((4, 16, C1), BF16)] * 2,
        *[v((2, 16, DC), BF16)] * 2, *[v((4, 16, DC), BF16)] * 2,
        v((2, DP, 16, C1), BF16), v((7, 16, C1), BF16), v((TM, 16, C1), BF16),
        pltpu.SemaphoreType.DMA((17,)), pltpu.SemaphoreType.DMA((125,)), pltpu.SemaphoreType.DMA((125,)),
    ]
    fine = jax.ShapeDtypeStruct((1, FINE, PIX, C1), BF16)
    ig, sums = pl.pallas_call(
        kernel,
        out_shape=(fine, jax.ShapeDtypeStruct((TM, 16, C1), BF16)),
        in_specs=[hbm] * 7,
        out_specs=(hbm, vmem),
        scratch_shapes=scratch,
        compiler_params=pltpu.CompilerParams(
            collective_id=0, has_side_effects=True, vmem_limit_bytes=60 * 1024 * 1024
        ),
        cost_estimate=pl.CostEstimate(flops=9 * 10**9, bytes_accessed=16 * 10**6, transcendentals=10**6),
    )(*args)
    return pl.pallas_call(
        finish,
        out_shape=(fine, jax.ShapeDtypeStruct((60, C1), F32), jax.ShapeDtypeStruct((20, C2), F32)),
        in_specs=[hbm, vmem],
        out_specs=(hbm, vmem, vmem),
        scratch_shapes=[pltpu.SemaphoreType.DMA],
        cost_estimate=pl.CostEstimate(flops=10**5, bytes_accessed=2 * 10**6, transcendentals=0),
    )(ig, sums)


def solution(mesh):
    fine, whole = P("dp", "tm", "space", None), P()
    rows = P(("space", "dp"), None)
    return jax.shard_map(
        shards,
        mesh=mesh,
        in_specs=(fine, whole, whole, whole, whole, fine, fine),
        out_specs=(fine, rows, rows),
        check_vma=False,
    )
```

time: 116 us -> 115 us (level)
  local copies, waits for them, and re-layouts: 5.38 us -> 0 us
  Pallas kernels: 109 us -> 114 us
    unnamed x3 -> x0, local copies, waits for them, and re-layouts: 5.38 us -> none
    pallas_call x1 -> x2, Pallas kernels: 109 us -> 114 us  [the longest x1 81.9 us: shards(): pl.pallas_call(kernel, out_shape=(fine, jax.ShapeDtypeStruct((TM, 16, C1)...]
where the time goes in v2:
time: 115 us
  Pallas kernels  114 us (99%)
    pallas_call x1, Pallas kernels, shards(): pl.pallas_call(kernel, out_shape=(fine, jax.ShapeDtypeStruct((TM, 16, C1)...  81.9 us
    pallas_call x1, Pallas kernels, shards(): pl.pallas_call(finish, out_shape=(fine, jax.ShapeDtypeStruct((60, C1), F3...  32.5 us

profile of v2, /device:TPU:2, one launch (start us, length us, event | category | flops | bytes accessed | tf_op | source)
XLA Modules:
  0.0 115.2 jit_solution(10922006147181850143)
XLA Ops:
  0.6 81.9 %shard_map.94 = (bf16[1,4,192,640]{3,2,1,0:T(8,128)(2,1)}, bf16[8,16,640]{2,1,0:T(8,128)(2,1)}) custom-call(bf16[1,4,192,640]{3,2,1,0:T(8,128)(2,1)} %frames.1, bf16[1920,640]{1,0:T(8,128)(2,1)} %w_time.1, bf16[640,1280]{1,0:T(8,128)(2,1)} %w_down.1, bf16[1280,1280]{1,0:T(8,128)(2,1)} %w_query.1, bf16[1280,1280]{1,0:T(8,128)(2,1)} %w_key.1, ...), custom_call_target="tpu_custom_call" | custom-call | flops 8999999488 | bytes 16000000 | tf_op jit(solution)/shard_map/pallas_call | solution.py:490
  82.6 32.5 %shard_map.95 = (bf16[1,4,192,640]{3,2,1,0:T(8,128)(2,1)}, f32[60,640]{1,0:T(8,128)}, f32[20,1280]{1,0:T(8,128)}) custom-call(bf16[1,4,192,640]{3,2,1,0:T(8,128)(2,1)} %get-tuple-element.5.ig, bf16[8,16,640]{2,1,0:T(8,128)(2,1)} %get-tuple-element.6.sums), custom_call_target="tpu_custom_call" | custom-call | flops 100000 | bytes 2000000 | tf_op jit(solution)/shard_map/pallas_call | solution.py:501

commit v3 on v2

--- a/solution.py
+++ b/solution.py
@@ -136,7 +136,7 @@
     ext, wt, wd, wq, wk, gs, go, pre, skipsum, work, qf, kf, cb, gb, bq, bk,
     g_send, g_recv, c_send, c_recv, b_send, b_recv, bc, spread, bpe,
     t_sum, d_sum, cs_y, cs_x, p_y, p_x, y_ra, y_rb, y_fp, y_fm, x_ra, x_rb, x_fp, x_fm,
-    p2_y, p2_x, y2_ra, y2_rb, y2_fp, y2_fm, x2_ra, x2_rb, x2_fp, x2_fm,
+    p2_y, p2_x, r2_y, r2_x,
     z_buf, z_recv, final,
     local_sem, send_sem, recv_sem,
 ):
@@ -164,19 +164,19 @@
             )
         )
     ]
-    for load in loads:
-        load.start()
+    loads[0].start()
+    loads[1].start()
 
     peers_tm = [at(tm_=(tm + k) % TM) for k in range(1, TM)]
     partner = at(space_=y * 2 + 1 - core)
-    y_plus, y_minus = (at(space_=((y + k) % YS) * 2 + core) for k in (1, 3))
-    x_plus, x_minus = (at(tm_=zlo * XS + (x + k) % XS) for k in (1, 3))
+    peers_y = [at(space_=((y + k) % YS) * 2 + core) for k in range(1, YS)]
+    peers_x = [at(tm_=zlo * XS + (x + k) % XS) for k in range(1, XS)]
     zpos = dp * 2 + zlo
     on_z = [(zpos + k) % 8 for k in range(1, 8)]
     peers_z = [at(tm_=z % 2 * XS + x, dp_=z // 2) for z in on_z]
     barrier = pltpu.get_barrier_semaphore()
     other_z = [at(tm_=tm_, dp_=(dp + k) % DP) for k in range(1, DP) for tm_ in (x, XS + x)]
-    greeted = peers_tm + [partner, y_plus, y_minus] + other_z
+    greeted = peers_tm + [partner] + peers_y + other_z
     for peer in greeted:
         pl.semaphore_signal(barrier, inc=1, device_id=peer, device_id_type=MESH)
     pl.semaphore_wait(barrier, len(greeted))
@@ -232,6 +232,8 @@
         first = send(remote(frames.at[0, 0, rows], ext.at[FINE + 1, rows], 72 + 2 * c, prev))
         last = send(remote(frames.at[0, FINE - 1, rows], ext.at[0, rows], 73 + 2 * c, nxt))
         halos.append((first, last))
+    for load in loads[2:]:
+        load.start()
 
     loads[0].wait()
     loads[1].wait()
@@ -324,26 +326,19 @@
         return jnp.concatenate([rows[:16], fold_tail(rows[16:]), jnp.zeros((16, 128), F32)], axis=1)
 
     swap_y = []
-    for part_y in range(YS):
-
-        def time_block(i, carry):
-            cols = pl.ds(pl.multiple_of(i % 5 * 128, 128), 128)
-            block = ext[pl.ds(i // 5, FINE), :, cols].reshape(FINE * PIX, 128)
-            start = pl.multiple_of(i * 128, 128)
-            t_sum[pl.ds(start, 128), :] = dot_first(block, bpe[1 : FINE + 1].reshape(FINE * PIX, C1))
-            return carry
-
-        lax.fori_loop(4 * part_y, min(4 * part_y + 4, 15), time_block, 0)
-        for h in range(DP):
-            cs_y[part_y, h] = time_unit(part_y, 1 - core, h).astype(BF16)
-        swap_y.append(send(remote(cs_y.at[part_y], p_y.at[part_y], 80 + part_y, partner)))
-
-    def down(i, carry):
-        cols = pl.ds(pl.multiple_of(i * 128, 128), 128)
-        d_sum[cols, :] = dot_first(skipsum[:, cols], bc[...])
-        return carry
-
-    lax.fori_loop(0, C1 // 128, down, 0)
+    back_rows = bpe[1 : FINE + 1].reshape(FINE * PIX, C1)
+    for k in range(3):
+        for lo, hi in COLS_FINE:
+            block = ext[k : k + FINE, :, lo:hi].reshape(FINE * PIX, hi - lo)
+            t_sum[k * C1 + lo : k * C1 + hi, :] = dot_first(block, back_rows)
+            part_y = len(swap_y)
+            if part_y < YS and k * C1 + hi >= 480 * (part_y + 1):
+                for h in range(DP):
+                    cs_y[part_y, h] = time_unit(part_y, 1 - core, h).astype(BF16)
+                swap_y.append(send(remote(cs_y.at[part_y], p_y.at[part_y], 80 + part_y, partner)))
+
+    for lo, hi in COLS_FINE:
+        d_sum[lo:hi, :] = dot_first(skipsum[:, lo:hi], bc[...])
 
     def pack_down(part_y, carry):
         for h in range(DP):
@@ -355,7 +350,7 @@
     lax.fori_loop(0, YS, pack_down, 0)
     swap_x = send(remote(cs_x, p_x, 84, partner))
 
-    ring_y = Ring(remote, p_y, (y_ra, y_rb, y_fp, y_fm), y, y_plus, y_minus, 86)
+    ring_y = Ring(remote, p_y, (y_ra, y_rb, y_fp, y_fm), y, peers_y[0], peers_y[2], 86)
     for part_y, copies in (
         (ring_y.far, ring_y.copies[:2]),
         (ring_y.ahead, ring_y.copies[2:3]),
@@ -379,7 +374,7 @@
         return carry
 
     lax.fori_loop(0, YS, add_down, 0)
-    ring_x = Ring(remote, p_x, (x_ra, x_rb, x_fp, x_fm), x, x_plus, x_minus, 92)
+    ring_x = Ring(remote, p_x, (x_ra, x_rb, x_fp, x_fm), x, peers_x[0], peers_x[2], 92)
     ring_x.start()
 
     back_first.wait_recv()
@@ -403,32 +398,28 @@
             gs[t : t + 2, :, lo:hi] = acc.astype(BF16)
 
     input_grad(*COLS_FINE[0])
+    input_grad(*COLS_FINE[1])
     ring_y.middle()
-    input_grad(*COLS_FINE[1])
+    input_grad(*COLS_FINE[2])
     ring_x.middle()
-    input_grad(*COLS_FINE[2])
     store = pltpu.make_async_copy(gs, ig_out.at[0], local_sem.at[16])
     store.start()
 
     ring_y.arrived()
     for h in range(DP):
         p2_y[:, h] = ring_y.total(h).astype(BF16).reshape(XS, 16, C1)
-    ring2_y = Ring(remote, p2_y, (y2_ra, y2_rb, y2_fp, y2_fm), x, x_plus, x_minus, 98)
-    ring2_y.start()
+    y_copies = [send(remote(p2_y.at[(x + k) % XS], r2_y.at[k - 1], 97 + k, peers_x[k - 1])) for k in range(1, XS)]
     ring_x.arrived()
     for part_y in range(YS):
         p2_x[part_y] = ring_x.total(part_y).astype(BF16)
-    ring2_x = Ring(remote, p2_x, (x2_ra, x2_rb, x2_fp, x2_fm), y, y_plus, y_minus, 104)
-    ring2_x.start()
-    ring2_y.middle()
-    ring2_x.middle()
-    ring2_y.arrived()
-    for h in range(DP):
-        z_buf[0, h] = ring2_y.total(h).astype(BF16)
-    ring2_x.arrived()
-    for h in range(DP):
-        z_buf[1, h, :, :DC] = ring2_x.total(h).astype(BF16)
-        z_buf[1, h, :, DC:] = jnp.zeros((16, C1 - DC), BF16)
+    x_copies = [send(remote(p2_x.at[(y + k) % YS], r2_x.at[k - 1], 100 + k, peers_y[k - 1])) for k in range(1, YS)]
+    for copy in y_copies:
+        copy.wait_recv()
+    z_buf[0] = (p2_y[x].astype(F32) + sum(r2_y[k].astype(F32) for k in range(XS - 1))).astype(BF16)
+    for copy in x_copies:
+        copy.wait_recv()
+    z_buf[1, :, :, :DC] = (p2_x[y].astype(F32) + sum(r2_x[k].astype(F32) for k in range(YS - 1))).astype(BF16)
+    z_buf[1, :, :, DC:] = jnp.zeros((DP, 16, C1 - DC), BF16)
 
     z_copies = [
         send(remote(z_buf.at[z % 2, z // 2], z_recv.at[k], 110 + k, peers_z[k])) for k, z in enumerate(on_z)
@@ -447,14 +438,16 @@
 
     for copy in sent:
         copy.wait_send()
-    for ring in (ring_x, ring_y, ring2_x, ring2_y):
+    for ring in (ring_x, ring_y):
         ring.finish()
     store.wait()
 
 
-def finish(ig, sums, ig_out, time_out, down_out, sem):
-    copy = pltpu.make_async_copy(ig, ig_out, sem)
-    copy.start()
+def finish(ig, sums, ig_out, time_out, down_out, held, load_sem, store_sem):
+    loads = [pltpu.make_async_copy(ig.at[0, t], held.at[t], load_sem.at[t]) for t in range(FINE)]
+    stores = [pltpu.make_async_copy(held.at[t], ig_out.at[0, t], store_sem.at[t]) for t in range(FINE)]
+    for load in loads:
+        load.start()
     odd = lax.axis_index("dp") % 2 == 1
     scale = 1.0 / math.sqrt(ROWS_ALL)
     rows = sums[:XS].astype(F32).reshape(64, C1) * scale
@@ -462,7 +455,11 @@
     wide = jnp.concatenate([sums[XS + part_x, :, :DC] for part_x in range(XS)], axis=1).astype(F32) * (0.25 * scale)
     rows = jnp.concatenate([wide[:, :C2], open_tail(wide[:, C2 : C2 + C1])], axis=0)
     down_out[...] = jnp.where(odd, rows[4:24], rows[:20])
-    copy.wait()
+    for load, store in zip(loads, stores):
+        load.wait()
+        store.start()
+    for store in stores:
+        store.wait()
 
 
 def shards(*args):
@@ -481,8 +478,7 @@
         *[v((2, 64, C1), BF16)] * 2, *[v((4, 64, C1), BF16)] * 2,
         *[v((2, DP, 16, DC), BF16)] * 2, *[v((4, DP, 16, DC), BF16)] * 2,
         v((XS, DP, 16, C1), BF16), v((YS, DP, 16, DC), BF16),
-        *[v((2, 16, C1), BF16)] * 2, *[v((4, 16, C1), BF16)] * 2,
-        *[v((2, 16, DC), BF16)] * 2, *[v((4, 16, DC), BF16)] * 2,
+        v((XS - 1, DP, 16, C1), BF16), v((YS - 1, DP, 16, DC), BF16),
         v((2, DP, 16, C1), BF16), v((7, 16, C1), BF16), v((TM, 16, C1), BF16),
         pltpu.SemaphoreType.DMA((17,)), pltpu.SemaphoreType.DMA((125,)), pltpu.SemaphoreType.DMA((125,)),
     ]
@@ -503,7 +499,11 @@
         out_shape=(fine, jax.ShapeDtypeStruct((60, C1), F32), jax.ShapeDtypeStruct((20, C2), F32)),
         in_specs=[hbm, vmem],
         out_specs=(hbm, vmem, vmem),
-        scratch_shapes=[pltpu.SemaphoreType.DMA],
+        scratch_shapes=[
+            v((FINE, PIX, C1), BF16),
+            pltpu.SemaphoreType.DMA((FINE,)),
+            pltpu.SemaphoreType.DMA((FINE,)),
+        ],
         cost_estimate=pl.CostEstimate(flops=10**5, bytes_accessed=2 * 10**6, transcendentals=0),
     )(ig, sums)
 

time: 115 us -> 83.5 us (0.73)
  Pallas kernels: 114 us -> 82.3 us
    pallas_call x1, Pallas kernels: 32.5 us -> 3.69 us  [shards(): pl.pallas_call(finish, out_shape=(fine, jax.ShapeDtypeStruct((60, C1), F3...]
    pallas_call x1, Pallas kernels: 81.9 us -> 78.6 us  [shards(): pl.pallas_call(kernel, out_shape=(fine, jax.ShapeDtypeStruct((TM, 16, C1)...]
where the time goes in v3:
time: 83.5 us; the launch traced here: 83.1 us
  Pallas kernels  82.3 us (99%)
    pallas_call x1, Pallas kernels, shards(): pl.pallas_call(kernel, out_shape=(fine, jax.ShapeDtypeStruct((TM, 16, C1)...  78.6 us
    pallas_call x1, Pallas kernels, shards(): pl.pallas_call(finish, out_shape=(fine, jax.ShapeDtypeStruct((60, C1), F3...  3.69 us

profile of v3, /device:TPU:2, one launch (start us, length us, event | category | flops | bytes accessed | tf_op | source)
XLA Modules:
  0.0 83.1 jit_solution(7340568042218301726)
XLA Ops:
  0.6 78.6 %shard_map.94 = (bf16[1,4,192,640]{3,2,1,0:T(8,128)(2,1)}, bf16[8,16,640]{2,1,0:T(8,128)(2,1)}) custom-call(bf16[1,4,192,640]{3,2,1,0:T(8,128)(2,1)} %frames.1, bf16[1920,640]{1,0:T(8,128)(2,1)} %w_time.1, bf16[640,1280]{1,0:T(8,128)(2,1)} %w_down.1, bf16[1280,1280]{1,0:T(8,128)(2,1)} %w_query.1, bf16[1280,1280]{1,0:T(8,128)(2,1)} %w_key.1, ...), custom_call_target="tpu_custom_call" | custom-call | flops 8999999488 | bytes 16000000 | tf_op jit(solution)/shard_map/pallas_call | solution.py:486
  79.3 3.7 %shard_map.95 = (bf16[1,4,192,640]{3,2,1,0:T(8,128)(2,1)}, f32[60,640]{1,0:T(8,128)}, f32[20,1280]{1,0:T(8,128)}) custom-call(bf16[1,4,192,640]{3,2,1,0:T(8,128)(2,1)} %get-tuple-element.5.ig, bf16[8,16,640]{2,1,0:T(8,128)(2,1)} %get-tuple-element.6.sums), custom_call_target="tpu_custom_call" | custom-call | flops 100000 | bytes 2000000 | tf_op jit(solution)/shard_map/pallas_call | solution.py:497

commit v4 on v3

--- a/solution.py
+++ b/solution.py
@@ -19,6 +19,7 @@
 CHUNKS, WIDE = 3, 64
 DC = 512
 TILES = 5
+PIECES = ((0, 384), (384, 640))
 
 
 def dot(left, right):
@@ -81,39 +82,59 @@
             copy.wait_send()
 
 
-def attend(tiles, qf, kf, cb, gb, work, bq, bk):
-    row_i = lax.broadcasted_iota(jnp.int32, (128, 128), 0)
-    col_i = lax.broadcasted_iota(jnp.int32, (128, 128), 1)
-    ones = ((row_i // DH) == (col_i // DH)).astype(F32).astype(BF16)
-    mask = ((row_i[:WIDE] % 8) == (col_i[:WIDE] % 8)).astype(F32)
-    left = (lax.broadcasted_iota(jnp.int32, (WIDE, 128), 1) < DH).astype(F32)
-    left_b, right_b = left.astype(BF16), (1.0 - left).astype(BF16)
-    count = len(tiles)
-    units = [(i, slice(WIDE * g, WIDE * g + WIDE)) for i in range(count) for g in range(CHUNKS)]
-    index = range(len(units))
-
-    def heads(rows):
-        return jnp.concatenate([rows * left_b, rows * right_b], axis=0)
+def attend_units(tiles):
+    return [(i, slice(WIDE * g, WIDE * g + WIDE)) for i in range(len(tiles)) for g in range(CHUNKS)]
+
+
+def pair_ones():
+    rows, cols = (lax.broadcasted_iota(jnp.int32, (128, 128), d) for d in (0, 1))
+    return ((rows // DH) == (cols // DH)).astype(F32).astype(BF16)
+
+
+def pair_left():
+    return (lax.broadcasted_iota(jnp.int32, (WIDE, 128), 1) < DH).astype(F32)
+
+
+def pair_rows(rows):
+    left = pair_left()
+    return jnp.concatenate([rows * left.astype(BF16), rows * (1.0 - left).astype(BF16)], axis=0)
+
+
+def head_sums(terms):
+    sums = dot(jnp.concatenate([term.astype(BF16) for term in terms], axis=0), pair_ones())
+    rows = terms[0].shape[0]
+    return [sums[rows * i : rows * i + rows] for i in range(len(terms))]
+
+
+def attend_scores(tiles, qf, kf, probs_ref, bq, bk):
+    row_i, col_i = (lax.broadcasted_iota(jnp.int32, (WIDE, 128), d) for d in (0, 1))
+    mask = ((row_i % 8) == (col_i % 8)).astype(F32)
+    count, units = len(tiles), attend_units(tiles)
+    q, k = [qf[:, c] for c in tiles], [kf[:, c] for c in tiles]
+    factors = [lax.rsqrt(total * (1.0 / DH) + EPS) for total in head_sums([v * v for v in q + k])]
+    qb = [(q[i] * factors[i]).astype(BF16) for i in range(count)]
+    kb = [(k[i] * factors[count + i]).astype(BF16) for i in range(count)]
+    for i, c in enumerate(tiles):
+        qf[:, c], kf[:, c] = factors[i], factors[count + i]
+        bq[:, c], bk[:, c] = qb[i], kb[i]
+    raised = [jnp.exp(dot_last(qb[i][rows], pair_rows(kb[i][rows])) * 0.125) * mask for i, rows in units]
+    for (i, rows), over, under in zip(units, raised, head_sums(raised)):
+        probs_ref[rows, tiles[i]] = over / under
+
+
+def attend_back(tiles, qf, kf, probs_ref, cb, gb, work, bq, bk):
+    units = attend_units(tiles)
+    index, left = range(len(units)), pair_left()
 
     def fold(both):
         return jnp.where(left > 0.5, both[:WIDE], both[WIDE:])
 
-    def head_sums(terms):
-        sums = dot(jnp.concatenate([term.astype(BF16) for term in terms], axis=0), ones)
-        rows = terms[0].shape[0]
-        return [sums[rows * i : rows * i + rows] for i in range(len(terms))]
-
-    q, k = [qf[:, c] for c in tiles], [kf[:, c] for c in tiles]
-    factors = [lax.rsqrt(total * (1.0 / DH) + EPS) for total in head_sums([v * v for v in q + k])]
-    rq, rk = factors[:count], factors[count:]
-    qb = [(q[i] * rq[i]).astype(BF16) for i in range(count)]
-    kb = [(k[i] * rk[i]).astype(BF16) for i in range(count)]
-    queries = [qb[i][rows] for i, rows in units]
-    keys = [heads(kb[i][rows]) for i, rows in units]
-    raised = [jnp.exp(dot_last(queries[n], keys[n]) * 0.125) * mask for n in index]
+    queries = [bq[rows, tiles[i]] for i, rows in units]
+    plain_keys = [bk[rows, tiles[i]] for i, rows in units]
+    keys = [pair_rows(rows) for rows in plain_keys]
     upstream = [gb[rows, tiles[i]] for i, rows in units]
-    back_probs = [dot_last(upstream[n], heads(cb[rows, tiles[i]])) for n, (i, rows) in enumerate(units)]
-    probs = [over / under for over, under in zip(raised, head_sums(raised))]
+    probs = [probs_ref[rows, tiles[i]] for i, rows in units]
+    back_probs = [dot_last(upstream[n], pair_rows(cb[rows, tiles[i]])) for n, (i, rows) in enumerate(units)]
     means = head_sums([p * b for p, b in zip(probs, back_probs)])
     scores = [(p * (b - m)).astype(BF16) for p, b, m in zip(probs, back_probs, means)]
     for n, (i, rows) in enumerate(units):
@@ -121,23 +142,23 @@
         work[rows, tiles[i]] = upstream[n].astype(F32) + values
     back_q = [dot(scores[n], keys[n]) * 0.125 for n in index]
     back_k = [fold(dot_first(scores[n], queries[n])) * 0.125 for n in index]
-    qn = [rows.astype(F32) for rows in queries]
-    kn = [kb[i][rows].astype(F32) for i, rows in units]
+    qn, kn = [rows.astype(F32) for rows in queries], [rows.astype(F32) for rows in plain_keys]
     mean_q = head_sums([b * v for b, v in zip(back_q, qn)])
     mean_k = head_sums([b * v for b, v in zip(back_k, kn)])
     for n, (i, rows) in enumerate(units):
-        bq[rows, tiles[i]] = (rq[i][rows] * (back_q[n] - qn[n] * (mean_q[n] * (1.0 / DH)))).astype(BF16)
-        bk[rows, tiles[i]] = (rk[i][rows] * (back_k[n] - kn[n] * (mean_k[n] * (1.0 / DH)))).astype(BF16)
+        c = tiles[i]
+        bq[rows, c] = (qf[rows, c] * (back_q[n] - qn[n] * (mean_q[n] * (1.0 / DH)))).astype(BF16)
+        bk[rows, c] = (kf[rows, c] * (back_k[n] - kn[n] * (mean_k[n] * (1.0 / DH)))).astype(BF16)
 
 
 def kernel(
     frames, w_time, w_down, w_query, w_key, grad_skip, grad_out,
-    ig_out, sums_out,
-    ext, wt, wd, wq, wk, gs, go, pre, skipsum, work, qf, kf, cb, gb, bq, bk,
-    g_send, g_recv, c_send, c_recv, b_send, b_recv, bc, spread, bpe,
-    t_sum, d_sum, cs_y, cs_x, p_y, p_x, y_ra, y_rb, y_fp, y_fm, x_ra, x_rb, x_fp, x_fm,
-    p2_y, p2_x, r2_y, r2_x,
-    z_buf, z_recv, final,
+    ig_out, time0_out, time1_out, down_out,
+    ext, wt, wd, wq, wk, gs, go, pre, skipsum, work, qf, kf, cb, gb, bq, bk, probs,
+    g_send, g_recv, c_send, c_recv, b_send, b_recv, bc, spread, bpe, t_sum, d_sum,
+    cs_0, p_0, ra_0, rb_0, fp_0, fm_0, p2_0, r2_0, zs_0, zr_0, f_0,
+    cs_1, p_1, ra_1, rb_1, fp_1, fm_1, p2_1, r2_1, zs_1, zr_1, f_1,
+    cs_x, p_x, x_ra, x_rb, x_fp, x_fm, p2_x, r2_x, zs_x, zr_x, f_x,
     local_sem, send_sem, recv_sem,
 ):
     tm, space, dp = lax.axis_index("tm"), lax.axis_index("space"), lax.axis_index("dp")
@@ -287,16 +308,22 @@
     for lo, hi in COLS_COARSE:
         qf[:, lo:hi] = dot(cb[...], wq[:, lo:hi])
         kf[:, lo:hi] = dot(cb[...], wk[:, lo:hi])
+    def tiles_of(i):
+        return [pl.ds(pl.multiple_of((i * TILES + u) * 128, 128), 128) for u in range(TILES)]
+
+    def some_scores(i, carry):
+        attend_scores(tiles_of(i), qf, kf, probs, bq, bk)
+        return carry
+
+    def some_back(i, carry):
+        attend_back(tiles_of(i), qf, kf, probs, cb, gb, work, bq, bk)
+        return carry
+
+    lax.fori_loop(0, C2 // 128 // TILES, some_scores, 0)
     for c in range(CHUNKS):
         g_receive[c]()
         unpack(g_recv, gb, c)
-
-    def attend_some(i, carry):
-        tiles = [pl.ds(pl.multiple_of((i * TILES + u) * 128, 128), 128) for u in range(TILES)]
-        attend(tiles, qf, kf, cb, gb, work, bq, bk)
-        return carry
-
-    lax.fori_loop(0, C2 // 128 // TILES, attend_some, 0)
+    lax.fori_loop(0, C2 // 128 // TILES, some_back, 0)
     for lo, hi in COLS_COARSE:
         work[:, lo:hi] += dot_last(bq[...], wq[lo:hi, :]) + dot_last(bk[...], wk[lo:hi, :])
     b_receive = []
@@ -316,27 +343,54 @@
     back_first = send(remote(bpe.at[1], bpe.at[FINE + 1], 78, prev))
     back_last = send(remote(bpe.at[FINE], bpe.at[0], 79, nxt))
 
-    def time_unit(part_y, part_core, part_dp):
+    def time_unit(part_y, part_core, part_dp, lo, hi):
         start = pl.multiple_of(480 * part_y + 240 * part_core + 60 * part_dp // 8 * 8, 8)
-        return t_sum[pl.ds(start, 64), :]
+        return t_sum[pl.ds(start, 64), lo:hi]
 
     def down_unit(part_y, part_core, part_dp):
         start = pl.multiple_of(160 * part_y + 80 * part_core + 20 * part_dp // 8 * 8, 8)
         rows = d_sum[pl.ds(start, 24), :]
         return jnp.concatenate([rows[:16], fold_tail(rows[16:]), jnp.zeros((16, 128), F32)], axis=1)
 
-    swap_y = []
-    back_rows = bpe[1 : FINE + 1].reshape(FINE * PIX, C1)
-    for k in range(3):
-        for lo, hi in COLS_FINE:
-            block = ext[k : k + FINE, :, lo:hi].reshape(FINE * PIX, hi - lo)
-            t_sum[k * C1 + lo : k * C1 + hi, :] = dot_first(block, back_rows)
-            part_y = len(swap_y)
-            if part_y < YS and k * C1 + hi >= 480 * (part_y + 1):
-                for h in range(DP):
-                    cs_y[part_y, h] = time_unit(part_y, 1 - core, h).astype(BF16)
-                swap_y.append(send(remote(cs_y.at[part_y], p_y.at[part_y], 80 + part_y, partner)))
-
+    cs, parts_t = (cs_0, cs_1), (p_0, p_1)
+    rings = [
+        Ring(remote, p_0, (ra_0, rb_0, fp_0, fm_0), y, peers_y[0], peers_y[2], 80),
+        Ring(remote, p_1, (ra_1, rb_1, fp_1, fm_1), y, peers_y[0], peers_y[2], 86),
+    ]
+
+    def time_grad(piece):
+        left, right = PIECES[piece]
+        back_rows = bpe[1 : FINE + 1, :, left:right].reshape(FINE * PIX, right - left)
+        part_y = 0
+        for k in range(3):
+            for lo, hi in COLS_FINE:
+                block = ext[k : k + FINE, :, lo:hi].reshape(FINE * PIX, hi - lo)
+                t_sum[k * C1 + lo : k * C1 + hi, left:right] = dot_first(block, back_rows)
+                if part_y < YS and k * C1 + hi >= 480 * (part_y + 1):
+                    for h in range(DP):
+                        cs[piece][part_y, h] = time_unit(part_y, 1 - core, h, left, right).astype(BF16)
+                    send(remote(cs[piece].at[part_y], parts_t[piece].at[part_y], 98 + 4 * piece + part_y, partner))
+                    part_y += 1
+
+    def time_ring(piece):
+        ring, parts = rings[piece], parts_t[piece]
+        for part_y, copies in (
+            (ring.far, ring.copies[:2]),
+            (ring.ahead, ring.copies[2:3]),
+            (ring.behind, ring.copies[3:4]),
+            (y, []),
+        ):
+            remote(cs[piece].at[part_y], parts.at[part_y], 98 + 4 * piece + part_y, partner).wait_recv()
+            for h in range(DP):
+                parts[part_y, h] = (
+                    parts[part_y, h].astype(F32) + time_unit(part_y, core, h, *PIECES[piece])
+                ).astype(BF16)
+            for copy in copies:
+                copy.start()
+
+    time_grad(0)
+    time_grad(1)
+    time_ring(0)
     for lo, hi in COLS_FINE:
         d_sum[lo:hi, :] = dot_first(skipsum[:, lo:hi], bc[...])
 
@@ -348,20 +402,8 @@
         return carry
 
     lax.fori_loop(0, YS, pack_down, 0)
-    swap_x = send(remote(cs_x, p_x, 84, partner))
-
-    ring_y = Ring(remote, p_y, (y_ra, y_rb, y_fp, y_fm), y, peers_y[0], peers_y[2], 86)
-    for part_y, copies in (
-        (ring_y.far, ring_y.copies[:2]),
-        (ring_y.ahead, ring_y.copies[2:3]),
-        (ring_y.behind, ring_y.copies[3:4]),
-        (y, []),
-    ):
-        remote(cs_y.at[part_y], p_y.at[part_y], 80 + part_y, partner).wait_recv()
-        for h in range(DP):
-            p_y[part_y, h] = (p_y[part_y, h].astype(F32) + time_unit(part_y, core, h)).astype(BF16)
-        for copy in copies:
-            copy.start()
+    swap_x = send(remote(cs_x, p_x, 106, partner))
+    time_ring(1)
 
     swap_x.wait_recv()
 
@@ -398,61 +440,134 @@
             gs[t : t + 2, :, lo:hi] = acc.astype(BF16)
 
     input_grad(*COLS_FINE[0])
+    rings[0].middle()
     input_grad(*COLS_FINE[1])
-    ring_y.middle()
+    rings[1].middle()
     input_grad(*COLS_FINE[2])
     ring_x.middle()
     store = pltpu.make_async_copy(gs, ig_out.at[0], local_sem.at[16])
     store.start()
 
-    ring_y.arrived()
-    for h in range(DP):
-        p2_y[:, h] = ring_y.total(h).astype(BF16).reshape(XS, 16, C1)
-    y_copies = [send(remote(p2_y.at[(x + k) % XS], r2_y.at[k - 1], 97 + k, peers_x[k - 1])) for k in range(1, XS)]
+    def over_x(piece, p2, r2, first):
+        ring = rings[piece]
+        ring.arrived()
+        for h in range(DP):
+            p2[:, h] = ring.total(h).astype(BF16).reshape(p2.shape[0], 16, p2.shape[3])
+        return [send(remote(p2.at[(x + k) % XS], r2.at[k - 1], first + k, peers_x[k - 1])) for k in range(1, XS)]
+
+    def added(copies, own, more):
+        for copy in copies:
+            copy.wait_recv()
+        return (own.astype(F32) + sum(more[k].astype(F32) for k in range(len(copies)))).astype(BF16)
+
+    last_waits = []
+
+    class OverZ:
+        def __init__(self, src, slots, first, owner):
+            self.src, self.slots, self.first, self.owner = src, slots, first, owner
+            other = zlo if owner == 0 else 1 - zlo
+            copies = []
+            for k in range(DP):
+                h = (dp + k) % DP
+                slot = other * DP + k
+                target = at(tm_=owner * XS + x, dp_=h)
+                copies.append(remote(src.at[h], slots.at[slot], first + k, target, landed=first + slot))
+            for copy in copies[1:]:
+                copy.start()
+
+            @pl.when(zlo != owner)
+            def _():
+                copies[0].start()
+
+            def finish():
+                for copy in copies[1:]:
+                    copy.wait_send()
+
+                @pl.when(zlo != owner)
+                def _():
+                    copies[0].wait_send()
+
+            last_waits.append(finish)
+
+        def gather(self, final, first):
+            copies = [
+                remote(final.at[x], final.at[x], first + k, peers_tm[k - 1], landed=first + TM + x)
+                for k in range(1, TM)
+            ]
+
+            @pl.when(zlo == self.owner)
+            def _():
+                total = self.src[dp].astype(F32)
+                for slot in range(1, 2 * DP):
+                    ref = self.slots.at[slot]
+                    remote(ref, ref, self.first + slot, partner).wait_recv()
+                    total += self.slots[slot].astype(F32)
+                final[x] = total.astype(BF16)
+                for copy in copies:
+                    copy.start()
+
+            def finish():
+                for k in range(1, XS):
+                    ref = final.at[(x + k) % XS]
+                    remote(ref, ref, first, partner, landed=first + TM + (x + k) % XS).wait_recv()
+
+                @pl.when(zlo != self.owner)
+                def _():
+                    remote(final.at[x], final.at[x], first, partner, landed=first + TM + x).wait_recv()
+
+                @pl.when(zlo == self.owner)
+                def _():
+                    for copy in copies:
+                        copy.wait_send()
+
+            last_waits.append(finish)
+
+    copies_0 = over_x(0, p2_0, r2_0, 107)
+    copies_1 = over_x(1, p2_1, r2_1, 110)
     ring_x.arrived()
     for part_y in range(YS):
         p2_x[part_y] = ring_x.total(part_y).astype(BF16)
-    x_copies = [send(remote(p2_x.at[(y + k) % YS], r2_x.at[k - 1], 100 + k, peers_y[k - 1])) for k in range(1, YS)]
-    for copy in y_copies:
-        copy.wait_recv()
-    z_buf[0] = (p2_y[x].astype(F32) + sum(r2_y[k].astype(F32) for k in range(XS - 1))).astype(BF16)
-    for copy in x_copies:
-        copy.wait_recv()
-    z_buf[1, :, :, :DC] = (p2_x[y].astype(F32) + sum(r2_x[k].astype(F32) for k in range(YS - 1))).astype(BF16)
-    z_buf[1, :, :, DC:] = jnp.zeros((DP, 16, C1 - DC), BF16)
-
+    copies_x = [send(remote(p2_x.at[(y + k) % YS], r2_x.at[k - 1], 113 + k, peers_y[k - 1])) for k in range(1, YS)]
+    zs_0[...] = added(copies_0, p2_0[x], r2_0)
+    over_z0 = OverZ(zs_0, zr_0, 117, 0)
+    zs_1[...] = added(copies_1, p2_1[x], r2_1)
+    over_z1 = OverZ(zs_1, zr_1, 125, 1)
+    sums = added(copies_x, p2_x[y], r2_x)
+    for half in range(2):
+        zs_x[half] = sums[:, :, half * DC // 2 : (half + 1) * DC // 2]
     z_copies = [
-        send(remote(z_buf.at[z % 2, z // 2], z_recv.at[k], 110 + k, peers_z[k])) for k, z in enumerate(on_z)
+        send(remote(zs_x.at[z % 2, z // 2], zr_x.at[k], 133 + k, peers_z[k])) for k, z in enumerate(on_z)
     ]
-    total = z_buf[zlo, dp].astype(F32)
-    for k in range(7):
-        z_copies[k].wait_recv()
-        total += z_recv[k].astype(F32)
-    final[tm] = total.astype(BF16)
+    over_z0.gather(f_0, 140)
+    over_z1.gather(f_1, 152)
+    f_x[tm] = added(z_copies, zs_x[zlo, dp], zr_x)
     for k in range(1, TM):
-        send(remote(final.at[tm], final.at[tm], 117 + k, peers_tm[k - 1]))
+        send(remote(f_x.at[tm], f_x.at[tm], 163 + k, peers_tm[k - 1]))
     for k in range(1, TM):
         src = (tm + TM - k) % TM
-        remote(final.at[src], final.at[src], 117 + k, at(tm_=src)).wait_recv()
-    sums_out[...] = final[...]
+        remote(f_x.at[src], f_x.at[src], 163 + k, at(tm_=src)).wait_recv()
+    for wait in last_waits:
+        wait()
+    time0_out[...], time1_out[...], down_out[...] = f_0[...], f_1[...], f_x[...]
 
     for copy in sent:
         copy.wait_send()
-    for ring in (ring_x, ring_y):
+    for ring in rings + [ring_x]:
         ring.finish()
     store.wait()
 
 
-def finish(ig, sums, ig_out, time_out, down_out, held, load_sem, store_sem):
+def finish(ig, time0, time1, down, ig_out, time_out, down_out, held, load_sem, store_sem):
     loads = [pltpu.make_async_copy(ig.at[0, t], held.at[t], load_sem.at[t]) for t in range(FINE)]
     stores = [pltpu.make_async_copy(held.at[t], ig_out.at[0, t], store_sem.at[t]) for t in range(FINE)]
     for load in loads:
         load.start()
     odd = lax.axis_index("dp") % 2 == 1
     scale = 1.0 / math.sqrt(ROWS_ALL)
-    rows = sums[:XS].astype(F32).reshape(64, C1) * scale
+    rows = jnp.concatenate([time0[...], time1[...]], axis=2).astype(F32).reshape(64, C1) * scale
     time_out[...] = jnp.where(odd, rows[4:64], rows[:60])
-    wide = jnp.concatenate([sums[XS + part_x, :, :DC] for part_x in range(XS)], axis=1).astype(F32) * (0.25 * scale)
+    halves = [down[half * XS + part_x] for part_x in range(XS) for half in range(2)]
+    wide = jnp.concatenate(halves, axis=1).astype(F32) * (0.25 * scale)
     rows = jnp.concatenate([wide[:, :C2], open_tail(wide[:, C2 : C2 + C1])], axis=0)
     down_out[...] = jnp.where(odd, rows[4:24], rows[:20])
     for load, store in zip(loads, stores):
@@ -462,6 +577,16 @@
         store.wait()
 
 
+def reduce_scratch(n):
+    v = pltpu.VMEM
+    return [
+        v((YS, DP, 64, n), BF16), v((YS, DP, 64, n), BF16),
+        v((2, 64, n), BF16), v((2, 64, n), BF16), v((4, 64, n), BF16), v((4, 64, n), BF16),
+        v((XS, DP, 16, n), BF16), v((XS - 1, DP, 16, n), BF16),
+        v((DP, 16, n), BF16), v((2 * DP, 16, n), BF16), v((XS, 16, n), BF16),
+    ]
+
+
 def shards(*args):
     v, hbm = pltpu.VMEM, pl.BlockSpec(memory_space=pl.ANY)
     vmem = pl.BlockSpec(memory_space=pltpu.VMEM)
@@ -469,25 +594,27 @@
         v((FINE + 2, PIX, C1), BF16), v((3 * C1, C1), BF16), v((C1, C2), BF16), v((C2, C2), BF16), v((C2, C2), BF16),
         v((FINE, PIX, C1), BF16), v((PIX, C2), BF16), v((FINE, PIX, C1), F32), v((PIX, C1), BF16),
         v((PIX, C2), F32), v((PIX, C2), F32), v((PIX, C2), F32),
-        v((PIX, C2), BF16), v((PIX, C2), BF16), v((PIX, C2), BF16), v((PIX, C2), BF16),
+        v((PIX, C2), BF16), v((PIX, C2), BF16), v((PIX, C2), BF16), v((PIX, C2), BF16), v((PIX, C2), F32),
         *[v((CHUNKS, TM, 16, C1), BF16)] * 6,
         v((PIX, C2), BF16), v((PIX, C1), F32), v((FINE + 2, PIX, C1), BF16),
         v((3 * C1, C1), F32), v((C1, C2), F32),
-        v((YS, DP, 64, C1), BF16), v((XS, YS, DP, 16, DC), BF16),
-        v((YS, DP, 64, C1), BF16), v((XS, YS, DP, 16, DC), BF16),
-        *[v((2, 64, C1), BF16)] * 2, *[v((4, 64, C1), BF16)] * 2,
+        *[s for lo, hi in PIECES for s in reduce_scratch(hi - lo)],
+        v((XS, YS, DP, 16, DC), BF16), v((XS, YS, DP, 16, DC), BF16),
         *[v((2, DP, 16, DC), BF16)] * 2, *[v((4, DP, 16, DC), BF16)] * 2,
-        v((XS, DP, 16, C1), BF16), v((YS, DP, 16, DC), BF16),
-        v((XS - 1, DP, 16, C1), BF16), v((YS - 1, DP, 16, DC), BF16),
-        v((2, DP, 16, C1), BF16), v((7, 16, C1), BF16), v((TM, 16, C1), BF16),
-        pltpu.SemaphoreType.DMA((17,)), pltpu.SemaphoreType.DMA((125,)), pltpu.SemaphoreType.DMA((125,)),
+        v((YS, DP, 16, DC), BF16), v((YS - 1, DP, 16, DC), BF16),
+        v((2, DP, 16, DC // 2), BF16), v((7, 16, DC // 2), BF16), v((TM, 16, DC // 2), BF16),
+        pltpu.SemaphoreType.DMA((17,)), pltpu.SemaphoreType.DMA((171,)), pltpu.SemaphoreType.DMA((171,)),
     ]
     fine = jax.ShapeDtypeStruct((1, FINE, PIX, C1), BF16)
-    ig, sums = pl.pallas_call(
+    ig, *sums = pl.pallas_call(
         kernel,
-        out_shape=(fine, jax.ShapeDtypeStruct((TM, 16, C1), BF16)),
+        out_shape=(
+            fine,
+            *[jax.ShapeDtypeStruct((XS, 16, hi - lo), BF16) for lo, hi in PIECES],
+            jax.ShapeDtypeStruct((TM, 16, DC // 2), BF16),
+        ),
         in_specs=[hbm] * 7,
-        out_specs=(hbm, vmem),
+        out_specs=(hbm, vmem, vmem, vmem),
         scratch_shapes=scratch,
         compiler_params=pltpu.CompilerParams(
             collective_id=0, has_side_effects=True, vmem_limit_bytes=60 * 1024 * 1024
@@ -497,7 +624,7 @@
     return pl.pallas_call(
         finish,
         out_shape=(fine, jax.ShapeDtypeStruct((60, C1), F32), jax.ShapeDtypeStruct((20, C2), F32)),
-        in_specs=[hbm, vmem],
+        in_specs=[hbm, vmem, vmem, vmem],
         out_specs=(hbm, vmem, vmem),
         scratch_shapes=[
             v((FINE, PIX, C1), BF16),
@@ -505,7 +632,7 @@
             pltpu.SemaphoreType.DMA((FINE,)),
         ],
         cost_estimate=pl.CostEstimate(flops=10**5, bytes_accessed=2 * 10**6, transcendentals=0),
-    )(ig, sums)
+    )(ig, *sums)
 
 
 def solution(mesh):

time: 83.5 us -> 83.8 us (level)
  no operation moved by 1% of the time
where the time goes in v4:
time: 83.8 us; the launch traced here: 83.6 us
  Pallas kernels  82.8 us (99%)
    pallas_call x1, Pallas kernels, shards(): pl.pallas_call(kernel, out_shape=(fine, *[jax.ShapeDtypeStruct((XS, 16, h...  79.1 us
    pallas_call x1, Pallas kernels, shards(): pl.pallas_call(finish, out_shape=(fine, jax.ShapeDtypeStruct((60, C1), F3...  3.66 us

profile of v4, /device:TPU:2, one launch (start us, length us, event | category | flops | bytes accessed | tf_op | source)
XLA Modules:
  0.0 83.6 jit_solution(13829935239111143767)
XLA Ops:
  0.6 79.1 %shard_map.94 = (bf16[1,4,192,640]{3,2,1,0:T(8,128)(2,1)}, bf16[4,16,384]{2,1,0:T(8,128)(2,1)}, bf16[4,16,256]{2,1,0:T(8,128)(2,1)}, bf16[8,16,256]{2,1,0:T(8,128)(2,1)}) custom-call(bf16[1,4,192,640]{3,2,1,0:T(8,128)(2,1)} %frames.1, bf16[1920,640]{1,0:T(8,128)(2,1)} %w_time.1, bf16[640,1280]{1,0:T(8,128)(2,1)} %w_down.1, bf16[1280,1280]{1,0:T(8,128)(2,1)} %w_query.1, ...), custom_call_target="tpu_custom_call" | custom-call | flops 8999999488 | bytes 16000000 | tf_op jit(solution)/shard_map/pallas_call | solution.py:609
  79.8 3.7 %shard_map.95 = (bf16[1,4,192,640]{3,2,1,0:T(8,128)(2,1)}, f32[60,640]{1,0:T(8,128)}, f32[20,1280]{1,0:T(8,128)}) custom-call(bf16[1,4,192,640]{3,2,1,0:T(8,128)(2,1)} %get-tuple-element.7.ig, bf16[4,16,384]{2,1,0:T(8,128)(2,1)} %get-tuple-element.8.time0, bf16[4,16,256]{2,1,0:T(8,128)(2,1)} %get-tuple-element.9.time1, ...), custom_call_target="tpu_custom_call" | custom-call | flops 100000 | bytes 2000000 | tf_op jit(solution)/shard_map/pallas_call | solution.py:624

commit v5 on v4

--- a/solution.py
+++ b/solution.py
@@ -17,6 +17,7 @@
 COLS_FINE = ((0, 256), (256, 512), (512, 640))
 COLS_COARSE = tuple((n, n + 256) for n in range(0, C2, 256))
 CHUNKS, WIDE = 3, 64
+FOLD = 384
 DC = 512
 TILES = 5
 PIECES = ((0, 384), (384, 640))
@@ -36,6 +37,15 @@
 
 def fold_tail(tail):
     return jnp.concatenate([tail[:, :C1], tail[:, C1:]], axis=0)
+
+
+def fold_fine(rows):
+    rest = jnp.concatenate([rows[:, FOLD:], jnp.zeros((8, 2 * FOLD - C1), F32)], axis=1)
+    return jnp.concatenate([rows[:, :FOLD], rest], axis=0)
+
+
+def open_fine(rows):
+    return jnp.concatenate([rows[:8], rows[8:, : C1 - FOLD]], axis=1)
 
 
 def open_tail(tail):
@@ -155,7 +165,7 @@
     frames, w_time, w_down, w_query, w_key, grad_skip, grad_out,
     ig_out, time0_out, time1_out, down_out,
     ext, wt, wd, wq, wk, gs, go, pre, skipsum, work, qf, kf, cb, gb, bq, bk, probs,
-    g_send, g_recv, c_send, c_recv, b_send, b_recv, bc, spread, bpe, t_sum, d_sum,
+    g_send, g_recv, c_send, c_recv, b_send, b_recv, sk, bc, spread, bpe, t_sum, d_sum,
     cs_0, p_0, ra_0, rb_0, fp_0, fm_0, p2_0, r2_0, zs_0, zr_0, f_0,
     cs_1, p_1, ra_1, rb_1, fp_1, fm_1, p2_1, r2_1, zs_1, zr_1, f_1,
     cs_x, p_x, x_ra, x_rb, x_fp, x_fm, p2_x, r2_x, zs_x, zr_x, f_x,
@@ -237,14 +247,14 @@
         sent.append(copy)
         return copy
 
-    def pack(src, dst, c):
-        rows = src[c * WIDE : (c + 1) * WIDE, :].astype(F32)
+    def pack(src, dst, c, fold, width):
+        rows = src[c * WIDE : (c + 1) * WIDE, :width].astype(F32)
         for f in range(TM):
-            dst[c, f] = fold_tail(rows[8 * f : 8 * f + 8]).astype(BF16)
-
-    def unpack(src, dst, c):
-        rows = [open_tail(src[c, f].astype(F32)) for f in range(TM)]
-        dst[c * WIDE : (c + 1) * WIDE, :] = jnp.concatenate(rows, axis=0).astype(BF16)
+            dst[c, f] = fold(rows[8 * f : 8 * f + 8]).astype(BF16)
+
+    def unpack(src, dst, c, unfold):
+        rows = [unfold(src[c, f].astype(F32)) for f in range(TM)]
+        dst[c * WIDE : (c + 1) * WIDE, :] = jnp.concatenate(rows, axis=0).astype(dst.dtype)
 
     prev, nxt = at(tm_=(tm + TM - 1) % TM), at(tm_=(tm + 1) % TM)
     halos = []
@@ -265,9 +275,8 @@
         pre[0:3, :, lo:hi] += dot(ext[2:5].reshape(3 * PIX, C1), wt[2 * C1 :, lo:hi]).reshape(3, PIX, n)
     loads[3].wait()
     for c in range(CHUNKS):
-        pack(go, g_send, c)
-
-    loads[2].wait()
+        pack(go, g_send, c, fold_tail, C2)
+
     c_receive, g_receive = [], []
     for c in range(CHUNKS):
         rows = slice(c * WIDE, (c + 1) * WIDE)
@@ -293,18 +302,19 @@
                 total = skip if total is None else total + skip
                 pre[t, rows, lo:hi] = logistic * (1.0 + act * (1.0 - logistic))
             skipsum[rows, lo:hi] = total.astype(BF16)
-        for lo, hi in COLS_COARSE:
-            work[rows, lo:hi] = 0.25 * dot(skipsum[rows, :], wd[:, lo:hi])
-        pack(work, c_send, c)
+        pack(skipsum, c_send, c, fold_fine, C1)
         c_receive.append(exchange(c_send, c_recv, c, 8 * c))
     for c in range(CHUNKS):
         g_receive.append(exchange(g_send, g_recv, c, 24 + 8 * c))
 
+    loads[2].wait()
     loads[4].wait()
     loads[5].wait()
     for c in range(CHUNKS):
         c_receive[c]()
-        unpack(c_recv, cb, c)
+        unpack(c_recv, sk, c, open_fine)
+    for lo, hi in COLS_COARSE:
+        cb[:, lo:hi] = (0.25 * dot(sk[...], wd[:, lo:hi])).astype(BF16)
     for lo, hi in COLS_COARSE:
         qf[:, lo:hi] = dot(cb[...], wq[:, lo:hi])
         kf[:, lo:hi] = dot(cb[...], wk[:, lo:hi])
@@ -322,26 +332,17 @@
     lax.fori_loop(0, C2 // 128 // TILES, some_scores, 0)
     for c in range(CHUNKS):
         g_receive[c]()
-        unpack(g_recv, gb, c)
+        unpack(g_recv, gb, c, open_tail)
     lax.fori_loop(0, C2 // 128 // TILES, some_back, 0)
     for lo, hi in COLS_COARSE:
-        work[:, lo:hi] += dot_last(bq[...], wq[lo:hi, :]) + dot_last(bk[...], wk[lo:hi, :])
+        projected = dot_last(bq[...], wq[lo:hi, :]) + dot_last(bk[...], wk[lo:hi, :])
+        bc[:, lo:hi] = (work[:, lo:hi] + projected).astype(BF16)
+    for lo, hi in COLS_FINE:
+        work[:, lo:hi] = 0.25 * dot_last(bc[...], wd[lo:hi, :])
     b_receive = []
     for c in range(CHUNKS):
-        pack(work, b_send, c)
+        pack(work, b_send, c, fold_fine, C1)
         b_receive.append(exchange(b_send, b_recv, c, 48 + 8 * c))
-    for c in range(CHUNKS):
-        b_receive[c]()
-        unpack(b_recv, bc, c)
-
-    loads[6].wait()
-    for lo, hi in COLS_FINE:
-        spread[:, lo:hi] = 0.25 * dot_last(bc[...], wd[lo:hi, :])
-        for t in range(FINE):
-            back = gs[t, :, lo:hi].astype(F32) + spread[:, lo:hi]
-            bpe[t + 1, :, lo:hi] = (back * pre[t, :, lo:hi]).astype(BF16)
-    back_first = send(remote(bpe.at[1], bpe.at[FINE + 1], 78, prev))
-    back_last = send(remote(bpe.at[FINE], bpe.at[0], 79, nxt))
 
     def time_unit(part_y, part_core, part_dp, lo, hi):
         start = pl.multiple_of(480 * part_y + 240 * part_core + 60 * part_dp // 8 * 8, 8)
@@ -352,13 +353,44 @@
         rows = d_sum[pl.ds(start, 24), :]
         return jnp.concatenate([rows[:16], fold_tail(rows[16:]), jnp.zeros((16, 128), F32)], axis=1)
 
-    cs, parts_t = (cs_0, cs_1), (p_0, p_1)
-    rings = [
-        Ring(remote, p_0, (ra_0, rb_0, fp_0, fm_0), y, peers_y[0], peers_y[2], 80),
-        Ring(remote, p_1, (ra_1, rb_1, fp_1, fm_1), y, peers_y[0], peers_y[2], 86),
-    ]
-
-    def time_grad(piece):
+    for lo, hi in COLS_FINE:
+        d_sum[lo:hi, :] = dot_first(sk[:, lo:hi], bc[...])
+
+    def pack_down(part_y, carry):
+        for h in range(DP):
+            unit = down_unit(part_y, 1 - core, h).astype(BF16)
+            for part_x in range(XS):
+                cs_x[part_x, part_y, h] = unit[:, DC * part_x : DC * part_x + DC]
+        return carry
+
+    def add_down(part_y, carry):
+        for h in range(DP):
+            unit = down_unit(part_y, core, h)
+            for part_x in range(XS):
+                more = unit[:, DC * part_x : DC * part_x + DC]
+                p_x[part_x, part_y, h] = (p_x[part_x, part_y, h].astype(F32) + more).astype(BF16)
+        return carry
+
+    lax.fori_loop(0, YS, pack_down, 0)
+    swap_x = send(remote(cs_x, p_x, 106, partner))
+    swap_x.wait_recv()
+    lax.fori_loop(0, YS, add_down, 0)
+    ring_x = Ring(remote, p_x, (x_ra, x_rb, x_fp, x_fm), x, peers_x[0], peers_x[2], 92)
+    ring_x.start()
+
+    loads[6].wait()
+    for c in range(CHUNKS):
+        b_receive[c]()
+        unpack(b_recv, spread, c, open_fine)
+    for lo, hi in COLS_FINE:
+        for t in range(FINE):
+            back = gs[t, :, lo:hi].astype(F32) + spread[:, lo:hi]
+            bpe[t + 1, :, lo:hi] = (back * pre[t, :, lo:hi]).astype(BF16)
+
+    ring_0 = Ring(remote, p_0, (ra_0, rb_0, fp_0, fm_0), y, peers_y[0], peers_y[2], 80)
+    ring_1 = Ring(remote, p_1, (ra_1, rb_1, fp_1, fm_1), x, peers_x[0], peers_x[2], 86)
+
+    def time_grad(piece, cs, parts, place):
         left, right = PIECES[piece]
         back_rows = bpe[1 : FINE + 1, :, left:right].reshape(FINE * PIX, right - left)
         part_y = 0
@@ -368,98 +400,67 @@
                 t_sum[k * C1 + lo : k * C1 + hi, left:right] = dot_first(block, back_rows)
                 if part_y < YS and k * C1 + hi >= 480 * (part_y + 1):
                     for h in range(DP):
-                        cs[piece][part_y, h] = time_unit(part_y, 1 - core, h, left, right).astype(BF16)
-                    send(remote(cs[piece].at[part_y], parts_t[piece].at[part_y], 98 + 4 * piece + part_y, partner))
+                        unit = time_unit(part_y, 1 - core, h, left, right).astype(BF16)
+                        cs[(*place(part_y), h)] = unit if piece == 0 else unit.reshape(XS, 16, right - left)
+                    at_y = place(part_y)
+                    send(remote(cs.at[at_y], parts.at[at_y], 98 + 4 * piece + part_y, partner))
                     part_y += 1
 
-    def time_ring(piece):
-        ring, parts = rings[piece], parts_t[piece]
-        for part_y, copies in (
-            (ring.far, ring.copies[:2]),
-            (ring.ahead, ring.copies[2:3]),
-            (ring.behind, ring.copies[3:4]),
-            (y, []),
-        ):
-            remote(cs[piece].at[part_y], parts.at[part_y], 98 + 4 * piece + part_y, partner).wait_recv()
-            for h in range(DP):
-                parts[part_y, h] = (
-                    parts[part_y, h].astype(F32) + time_unit(part_y, core, h, *PIECES[piece])
-                ).astype(BF16)
-            for copy in copies:
-                copy.start()
-
-    time_grad(0)
-    time_grad(1)
-    time_ring(0)
-    for lo, hi in COLS_FINE:
-        d_sum[lo:hi, :] = dot_first(skipsum[:, lo:hi], bc[...])
-
-    def pack_down(part_y, carry):
+    time_grad(0, cs_0, p_0, lambda part_y: (part_y,))
+    ring_x.middle()
+    for part_y, copies in (
+        (ring_0.far, ring_0.copies[:2]),
+        (ring_0.ahead, ring_0.copies[2:3]),
+        (ring_0.behind, ring_0.copies[3:4]),
+        (y, []),
+    ):
+        remote(cs_0.at[part_y], p_0.at[part_y], 98 + part_y, partner).wait_recv()
         for h in range(DP):
-            unit = down_unit(part_y, 1 - core, h).astype(BF16)
-            for part_x in range(XS):
-                cs_x[part_x, part_y, h] = unit[:, DC * part_x : DC * part_x + DC]
-        return carry
-
-    lax.fori_loop(0, YS, pack_down, 0)
-    swap_x = send(remote(cs_x, p_x, 106, partner))
-    time_ring(1)
-
-    swap_x.wait_recv()
-
-    def add_down(part_y, carry):
+            p_0[part_y, h] = (p_0[part_y, h].astype(F32) + time_unit(part_y, core, h, *PIECES[0])).astype(BF16)
+        for copy in copies:
+            copy.start()
+
+    time_grad(1, cs_1, p_1, lambda part_y: (slice(None), part_y))
+    for part_y in range(YS):
+        remote(cs_1.at[:, part_y], p_1.at[:, part_y], 102 + part_y, partner).wait_recv()
         for h in range(DP):
-            unit = down_unit(part_y, core, h)
-            for part_x in range(XS):
-                more = unit[:, DC * part_x : DC * part_x + DC]
-                p_x[part_x, part_y, h] = (p_x[part_x, part_y, h].astype(F32) + more).astype(BF16)
-        return carry
-
-    lax.fori_loop(0, YS, add_down, 0)
-    ring_x = Ring(remote, p_x, (x_ra, x_rb, x_fp, x_fm), x, peers_x[0], peers_x[2], 92)
-    ring_x.start()
-
-    back_first.wait_recv()
-    back_last.wait_recv()
-
-    @pl.when(tm == 0)
-    def _():
-        bpe[0] = jnp.zeros((PIX, C1), BF16)
-
-    @pl.when(tm == TM - 1)
-    def _():
-        bpe[FINE + 1] = jnp.zeros((PIX, C1), BF16)
-
-    def input_grad(lo, hi):
-        for t in range(0, FINE, 2):
-            rows = [bpe[t + k : t + k + 2].reshape(2 * PIX, C1) for k in range(3)]
-            acc = dot_last(rows[2], wt[lo:hi, :])
-            acc += dot_last(rows[1], wt[C1 + lo : C1 + hi, :])
-            acc += dot_last(rows[0], wt[2 * C1 + lo : 2 * C1 + hi, :])
-            acc = acc.reshape(2, PIX, hi - lo) + gs[t : t + 2, :, lo:hi].astype(F32) + spread[:, lo:hi]
-            gs[t : t + 2, :, lo:hi] = acc.astype(BF16)
-
-    input_grad(*COLS_FINE[0])
-    rings[0].middle()
-    input_grad(*COLS_FINE[1])
-    rings[1].middle()
-    input_grad(*COLS_FINE[2])
-    ring_x.middle()
-    store = pltpu.make_async_copy(gs, ig_out.at[0], local_sem.at[16])
-    store.start()
-
-    def over_x(piece, p2, r2, first):
-        ring = rings[piece]
-        ring.arrived()
-        for h in range(DP):
-            p2[:, h] = ring.total(h).astype(BF16).reshape(p2.shape[0], 16, p2.shape[3])
-        return [send(remote(p2.at[(x + k) % XS], r2.at[k - 1], first + k, peers_x[k - 1])) for k in range(1, XS)]
+            unit = time_unit(part_y, core, h, *PIECES[1]).reshape(XS, 16, -1)
+            p_1[:, part_y, h] = (p_1[:, part_y, h].astype(F32) + unit).astype(BF16)
+    ring_1.start()
+
+    def input_grad(t, count, lo, hi):
+        rows = [bpe[t + k : t + k + count].reshape(count * PIX, C1) for k in range(3)]
+        acc = dot_last(rows[2], wt[lo:hi, :])
+        acc += dot_last(rows[1], wt[C1 + lo : C1 + hi, :])
+        acc += dot_last(rows[0], wt[2 * C1 + lo : 2 * C1 + hi, :])
+        acc = acc.reshape(count, PIX, hi - lo) + gs[t : t + count, :, lo:hi].astype(F32) + spread[:, lo:hi]
+        gs[t : t + count, :, lo:hi] = acc.astype(BF16)
+
+    input_grad(1, 2, *COLS_FINE[0])
+    ring_0.middle()
+    input_grad(1, 2, *COLS_FINE[1])
+    ring_1.middle()
+    back_first = send(remote(bpe.at[1], bpe.at[FINE + 1], 78, prev))
+    back_last = send(remote(bpe.at[FINE], bpe.at[0], 79, nxt))
+    input_grad(1, 2, *COLS_FINE[2])
 
     def added(copies, own, more):
         for copy in copies:
             copy.wait_recv()
         return (own.astype(F32) + sum(more[k].astype(F32) for k in range(len(copies)))).astype(BF16)
 
+    ring_x.arrived()
+    for part_y in range(YS):
+        p2_x[part_y] = ring_x.total(part_y).astype(BF16)
+    copies_x = [send(remote(p2_x.at[(y + k) % YS], r2_x.at[k - 1], 113 + k, peers_y[k - 1])) for k in range(1, YS)]
+    ring_0.arrived()
+    for h in range(DP):
+        p2_0[:, h] = ring_0.total(h).astype(BF16).reshape(XS, 16, -1)
+    copies_0 = [send(remote(p2_0.at[(x + k) % XS], r2_0.at[k - 1], 107 + k, peers_x[k - 1])) for k in range(1, XS)]
+    ring_1.arrived()
+    for part_y in range(YS):
+        p2_1[part_y] = ring_1.total(part_y).astype(BF16)
+    copies_1 = [send(remote(p2_1.at[(y + k) % YS], r2_1.at[k - 1], 110 + k, peers_y[k - 1])) for k in range(1, YS)]
     last_waits = []
 
     class OverZ:
@@ -522,27 +523,39 @@
 
             last_waits.append(finish)
 
-    copies_0 = over_x(0, p2_0, r2_0, 107)
-    copies_1 = over_x(1, p2_1, r2_1, 110)
-    ring_x.arrived()
-    for part_y in range(YS):
-        p2_x[part_y] = ring_x.total(part_y).astype(BF16)
-    copies_x = [send(remote(p2_x.at[(y + k) % YS], r2_x.at[k - 1], 113 + k, peers_y[k - 1])) for k in range(1, YS)]
-    zs_0[...] = added(copies_0, p2_0[x], r2_0)
-    over_z0 = OverZ(zs_0, zr_0, 117, 0)
-    zs_1[...] = added(copies_1, p2_1[x], r2_1)
-    over_z1 = OverZ(zs_1, zr_1, 125, 1)
     sums = added(copies_x, p2_x[y], r2_x)
     for half in range(2):
         zs_x[half] = sums[:, :, half * DC // 2 : (half + 1) * DC // 2]
     z_copies = [
         send(remote(zs_x.at[z % 2, z // 2], zr_x.at[k], 133 + k, peers_z[k])) for k, z in enumerate(on_z)
     ]
-    over_z0.gather(f_0, 140)
-    over_z1.gather(f_1, 152)
+    zs_0[...] = added(copies_0, p2_0[x], r2_0)
+    over_z0 = OverZ(zs_0, zr_0, 117, 0)
+    zs_1[...] = added(copies_1, p2_1[y], r2_1)
+    over_z1 = OverZ(zs_1, zr_1, 125, 1)
+
+    back_first.wait_recv()
+    back_last.wait_recv()
+
+    @pl.when(tm == 0)
+    def _():
+        bpe[0] = jnp.zeros((PIX, C1), BF16)
+
+    @pl.when(tm == TM - 1)
+    def _():
+        bpe[FINE + 1] = jnp.zeros((PIX, C1), BF16)
+
+    for lo, hi in COLS_FINE:
+        input_grad(0, 1, lo, hi)
+        input_grad(3, 1, lo, hi)
+    store = pltpu.make_async_copy(gs, ig_out.at[0], local_sem.at[16])
+    store.start()
+
     f_x[tm] = added(z_copies, zs_x[zlo, dp], zr_x)
     for k in range(1, TM):
         send(remote(f_x.at[tm], f_x.at[tm], 163 + k, peers_tm[k - 1]))
+    over_z0.gather(f_0, 140)
+    over_z1.gather(f_1, 152)
     for k in range(1, TM):
         src = (tm + TM - k) % TM
         remote(f_x.at[src], f_x.at[src], 163 + k, at(tm_=src)).wait_recv()
@@ -552,7 +565,7 @@
 
     for copy in sent:
         copy.wait_send()
-    for ring in rings + [ring_x]:
+    for ring in (ring_0, ring_1, ring_x):
         ring.finish()
     store.wait()
 
@@ -577,12 +590,22 @@
         store.wait()
 
 
-def reduce_scratch(n):
+def first_over_y(n):
     v = pltpu.VMEM
     return [
         v((YS, DP, 64, n), BF16), v((YS, DP, 64, n), BF16),
         v((2, 64, n), BF16), v((2, 64, n), BF16), v((4, 64, n), BF16), v((4, 64, n), BF16),
         v((XS, DP, 16, n), BF16), v((XS - 1, DP, 16, n), BF16),
+        v((DP, 16, n), BF16), v((2 * DP, 16, n), BF16), v((XS, 16, n), BF16),
+    ]
+
+
+def first_over_x(n):
+    v = pltpu.VMEM
+    return [
+        v((XS, YS, DP, 16, n), BF16), v((XS, YS, DP, 16, n), BF16),
+        v((2, DP, 16, n), BF16), v((2, DP, 16, n), BF16), v((4, DP, 16, n), BF16), v((4, DP, 16, n), BF16),
+        v((YS, DP, 16, n), BF16), v((YS - 1, DP, 16, n), BF16),
         v((DP, 16, n), BF16), v((2 * DP, 16, n), BF16), v((XS, 16, n), BF16),
     ]
 
@@ -595,10 +618,10 @@
         v((FINE, PIX, C1), BF16), v((PIX, C2), BF16), v((FINE, PIX, C1), F32), v((PIX, C1), BF16),
         v((PIX, C2), F32), v((PIX, C2), F32), v((PIX, C2), F32),
         v((PIX, C2), BF16), v((PIX, C2), BF16), v((PIX, C2), BF16), v((PIX, C2), BF16), v((PIX, C2), F32),
-        *[v((CHUNKS, TM, 16, C1), BF16)] * 6,
-        v((PIX, C2), BF16), v((PIX, C1), F32), v((FINE + 2, PIX, C1), BF16),
+        *[v((CHUNKS, TM, 16, C1), BF16)] * 2, *[v((CHUNKS, TM, 16, FOLD), BF16)] * 4,
+        v((PIX, C1), BF16), v((PIX, C2), BF16), v((PIX, C1), F32), v((FINE + 2, PIX, C1), BF16),
         v((3 * C1, C1), F32), v((C1, C2), F32),
-        *[s for lo, hi in PIECES for s in reduce_scratch(hi - lo)],
+        *first_over_y(PIECES[0][1] - PIECES[0][0]), *first_over_x(PIECES[1][1] - PIECES[1][0]),
         v((XS, YS, DP, 16, DC), BF16), v((XS, YS, DP, 16, DC), BF16),
         *[v((2, DP, 16, DC), BF16)] * 2, *[v((4, DP, 16, DC), BF16)] * 2,
         v((YS, DP, 16, DC), BF16), v((YS - 1, DP, 16, DC), BF16),

time: 83.8 us -> 78.3 us (0.934)
  Pallas kernels: 82.8 us -> 77.3 us
    pallas_call x1, Pallas kernels: 79.1 us -> 73.7 us  [shards(): pl.pallas_call(kernel, out_shape=(fine, *[jax.ShapeDtypeStruct((XS, 16, h...]
where the time goes in v5:
time: 78.3 us; the launch traced here: 78.1 us
  Pallas kernels  77.3 us (99%)
  between operations  0.8 us (1%)
    pallas_call x1, Pallas kernels, shards(): pl.pallas_call(kernel, out_shape=(fine, *[jax.ShapeDtypeStruct((XS, 16, h...  73.7 us
    pallas_call x1, Pallas kernels, shards(): pl.pallas_call(finish, out_shape=(fine, jax.ShapeDtypeStruct((60, C1), F3...  3.66 us

profile of v5, /device:TPU:2, one launch (start us, length us, event | category | flops | bytes accessed | tf_op | source)
XLA Modules:
  0.0 78.1 jit_solution(11381683496219691525)
XLA Ops:
  0.6 73.7 %shard_map.94 = (bf16[1,4,192,640]{3,2,1,0:T(8,128)(2,1)}, bf16[4,16,384]{2,1,0:T(8,128)(2,1)}, bf16[4,16,256]{2,1,0:T(8,128)(2,1)}, bf16[8,16,256]{2,1,0:T(8,128)(2,1)}) custom-call(bf16[1,4,192,640]{3,2,1,0:T(8,128)(2,1)} %frames.1, bf16[1920,640]{1,0:T(8,128)(2,1)} %w_time.1, bf16[640,1280]{1,0:T(8,128)(2,1)} %w_down.1, bf16[1280,1280]{1,0:T(8,128)(2,1)} %w_query.1, ...), custom_call_target="tpu_custom_call" | custom-call | flops 8999999488 | bytes 16000000 | tf_op jit(solution)/shard_map/pallas_call | solution.py:632
  74.3 3.7 %shard_map.95 = (bf16[1,4,192,640]{3,2,1,0:T(8,128)(2,1)}, f32[60,640]{1,0:T(8,128)}, f32[20,1280]{1,0:T(8,128)}) custom-call(bf16[1,4,192,640]{3,2,1,0:T(8,128)(2,1)} %get-tuple-element.7.ig, bf16[4,16,384]{2,1,0:T(8,128)(2,1)} %get-tuple-element.8.time0, bf16[4,16,256]{2,1,0:T(8,128)(2,1)} %get-tuple-element.9.time1, ...), custom_call_target="tpu_custom_call" | custom-call | flops 100000 | bytes 2000000 | tf_op jit(solution)/shard_map/pallas_call | solution.py:647

commit v6 on v5

--- a/solution.py
+++ b/solution.py
@@ -20,7 +20,7 @@
 FOLD = 384
 DC = 512
 TILES = 5
-PIECES = ((0, 384), (384, 640))
+PIECES = ((0, 256), (256, 512), (512, 640))
 
 
 def dot(left, right):
@@ -163,11 +163,12 @@
 
 def kernel(
     frames, w_time, w_down, w_query, w_key, grad_skip, grad_out,
-    ig_out, time0_out, time1_out, down_out,
+    ig_out, time0_out, time1_out, time2_out, down_out,
     ext, wt, wd, wq, wk, gs, go, pre, skipsum, work, qf, kf, cb, gb, bq, bk, probs,
     g_send, g_recv, c_send, c_recv, b_send, b_recv, sk, bc, spread, bpe, t_sum, d_sum,
-    cs_0, p_0, ra_0, rb_0, fp_0, fm_0, p2_0, r2_0, zs_0, zr_0, f_0,
-    cs_1, p_1, ra_1, rb_1, fp_1, fm_1, p2_1, r2_1, zs_1, zr_1, f_1,
+    cs_0, p_0, r_0, p2_0, r2_0, zs_0, zr_0, f_0,
+    cs_1, p_1, r_1, p2_1, r2_1, zs_1, zr_1, f_1,
+    cs_2, p_2, zr_2, p2_2, r2_2, xs_2, f_2,
     cs_x, p_x, x_ra, x_rb, x_fp, x_fm, p2_x, r2_x, zs_x, zr_x, f_x,
     local_sem, send_sem, recv_sem,
 ):
@@ -277,7 +278,7 @@
     for c in range(CHUNKS):
         pack(go, g_send, c, fold_tail, C2)
 
-    c_receive, g_receive = [], []
+    c_receive, g_receive = [], [exchange(g_send, g_recv, 0, 24)]
     for c in range(CHUNKS):
         rows = slice(c * WIDE, (c + 1) * WIDE)
         for copy in halos[c]:
@@ -304,7 +305,7 @@
             skipsum[rows, lo:hi] = total.astype(BF16)
         pack(skipsum, c_send, c, fold_fine, C1)
         c_receive.append(exchange(c_send, c_recv, c, 8 * c))
-    for c in range(CHUNKS):
+    for c in range(1, CHUNKS):
         g_receive.append(exchange(g_send, g_recv, c, 24 + 8 * c))
 
     loads[2].wait()
@@ -387,10 +388,7 @@
             back = gs[t, :, lo:hi].astype(F32) + spread[:, lo:hi]
             bpe[t + 1, :, lo:hi] = (back * pre[t, :, lo:hi]).astype(BF16)
 
-    ring_0 = Ring(remote, p_0, (ra_0, rb_0, fp_0, fm_0), y, peers_y[0], peers_y[2], 80)
-    ring_1 = Ring(remote, p_1, (ra_1, rb_1, fp_1, fm_1), x, peers_x[0], peers_x[2], 86)
-
-    def time_grad(piece, cs, parts, place):
+    def time_grad(piece, cs, parts, place, shape):
         left, right = PIECES[piece]
         back_rows = bpe[1 : FINE + 1, :, left:right].reshape(FINE * PIX, right - left)
         part_y = 0
@@ -401,32 +399,49 @@
                 if part_y < YS and k * C1 + hi >= 480 * (part_y + 1):
                     for h in range(DP):
                         unit = time_unit(part_y, 1 - core, h, left, right).astype(BF16)
-                        cs[(*place(part_y), h)] = unit if piece == 0 else unit.reshape(XS, 16, right - left)
-                    at_y = place(part_y)
-                    send(remote(cs.at[at_y], parts.at[at_y], 98 + 4 * piece + part_y, partner))
+                        cs[place(part_y, h)] = unit.reshape(*shape, right - left)
+                    if piece < 2:
+                        at_y = place(part_y, slice(None))
+                        send(remote(cs.at[at_y], parts.at[at_y], 98 + 4 * piece + part_y, partner))
                     part_y += 1
 
-    time_grad(0, cs_0, p_0, lambda part_y: (part_y,))
+    def add_time(piece, parts, place, shape, part_y):
+        left, right = PIECES[piece]
+        for h in range(DP):
+            unit = time_unit(part_y, core, h, left, right).reshape(*shape, right - left)
+            parts[place(part_y, h)] = (parts[place(part_y, h)].astype(F32) + unit).astype(BF16)
+
+    def by_y(part_y, h):
+        return (part_y, h)
+
+    def by_x(part_y, h):
+        return (slice(None), part_y, h)
+
+    def by_z(part_y, h):
+        return (h, slice(None), part_y)
+
+    time_grad(0, cs_0, p_0, by_y, (64,))
     ring_x.middle()
-    for part_y, copies in (
-        (ring_0.far, ring_0.copies[:2]),
-        (ring_0.ahead, ring_0.copies[2:3]),
-        (ring_0.behind, ring_0.copies[3:4]),
-        (y, []),
-    ):
+    time_grad(1, cs_1, p_1, by_x, (XS, 16))
+    copies_0 = []
+    for k in (2, 1, 3, 0):
+        part_y = (y + k) % YS
         remote(cs_0.at[part_y], p_0.at[part_y], 98 + part_y, partner).wait_recv()
-        for h in range(DP):
-            p_0[part_y, h] = (p_0[part_y, h].astype(F32) + time_unit(part_y, core, h, *PIECES[0])).astype(BF16)
-        for copy in copies:
-            copy.start()
-
-    time_grad(1, cs_1, p_1, lambda part_y: (slice(None), part_y))
+        add_time(0, p_0, by_y, (64,), part_y)
+        if k > 0:
+            copies_0.append(send(remote(p_0.at[part_y], r_0.at[k - 1], 79 + k, peers_y[k - 1])))
+    time_grad(2, cs_2, p_2, by_z, (2, 32))
+    swap_2 = send(remote(cs_2, p_2, 107, partner))
     for part_y in range(YS):
         remote(cs_1.at[:, part_y], p_1.at[:, part_y], 102 + part_y, partner).wait_recv()
-        for h in range(DP):
-            unit = time_unit(part_y, core, h, *PIECES[1]).reshape(XS, 16, -1)
-            p_1[:, part_y, h] = (p_1[:, part_y, h].astype(F32) + unit).astype(BF16)
-    ring_1.start()
+        add_time(1, p_1, by_x, (XS, 16), part_y)
+    copies_1 = [
+        send(remote(p_1.at[(x + k) % XS], r_1.at[k - 1], 82 + k, peers_x[k - 1])) for k in (2, 1, 3)
+    ]
+    swap_2.wait_recv()
+    for part_y in range(YS):
+        add_time(2, p_2, by_z, (2, 32), part_y)
+    copies_2 = [send(remote(p_2.at[z // 2, z % 2], zr_2.at[k], 171 + k, peers_z[k])) for k, z in enumerate(on_z)]
 
     def input_grad(t, count, lo, hi):
         rows = [bpe[t + k : t + k + count].reshape(count * PIX, C1) for k in range(3)]
@@ -436,31 +451,35 @@
         acc = acc.reshape(count, PIX, hi - lo) + gs[t : t + count, :, lo:hi].astype(F32) + spread[:, lo:hi]
         gs[t : t + count, :, lo:hi] = acc.astype(BF16)
 
-    input_grad(1, 2, *COLS_FINE[0])
-    ring_0.middle()
-    input_grad(1, 2, *COLS_FINE[1])
-    ring_1.middle()
-    back_first = send(remote(bpe.at[1], bpe.at[FINE + 1], 78, prev))
-    back_last = send(remote(bpe.at[FINE], bpe.at[0], 79, nxt))
-    input_grad(1, 2, *COLS_FINE[2])
-
-    def added(copies, own, more):
+    def arrived(copies):
         for copy in copies:
             copy.wait_recv()
+
+    def added(copies, own, more):
+        arrived(copies)
         return (own.astype(F32) + sum(more[k].astype(F32) for k in range(len(copies)))).astype(BF16)
 
+    input_grad(1, 2, *COLS_FINE[0])
     ring_x.arrived()
     for part_y in range(YS):
         p2_x[part_y] = ring_x.total(part_y).astype(BF16)
     copies_x = [send(remote(p2_x.at[(y + k) % YS], r2_x.at[k - 1], 113 + k, peers_y[k - 1])) for k in range(1, YS)]
-    ring_0.arrived()
+    input_grad(1, 2, *COLS_FINE[1])
+    input_grad(1, 2, *COLS_FINE[2])
+    arrived(copies_0)
     for h in range(DP):
-        p2_0[:, h] = ring_0.total(h).astype(BF16).reshape(XS, 16, -1)
+        total = p_0[y, h].astype(F32) + sum(r_0[k, h].astype(F32) for k in range(YS - 1))
+        p2_0[:, h] = total.astype(BF16).reshape(XS, 16, -1)
     copies_0 = [send(remote(p2_0.at[(x + k) % XS], r2_0.at[k - 1], 107 + k, peers_x[k - 1])) for k in range(1, XS)]
-    ring_1.arrived()
+    arrived(copies_1)
     for part_y in range(YS):
-        p2_1[part_y] = ring_1.total(part_y).astype(BF16)
+        p2_1[part_y] = (p_1[x, part_y].astype(F32) + sum(r_1[k, part_y].astype(F32) for k in range(XS - 1))).astype(BF16)
     copies_1 = [send(remote(p2_1.at[(y + k) % YS], r2_1.at[k - 1], 110 + k, peers_y[k - 1])) for k in range(1, YS)]
+    back_first = send(remote(bpe.at[1], bpe.at[FINE + 1], 78, prev))
+    back_last = send(remote(bpe.at[FINE], bpe.at[0], 79, nxt))
+    p2_2[...] = added(copies_2, p_2[dp, zlo], zr_2)
+    copies_2 = [send(remote(p2_2.at[(y + k) % YS], r2_2.at[k - 1], 177 + k, peers_y[k - 1])) for k in range(1, YS)]
+
     last_waits = []
 
     class OverZ:
@@ -534,6 +553,10 @@
     zs_1[...] = added(copies_1, p2_1[y], r2_1)
     over_z1 = OverZ(zs_1, zr_1, 125, 1)
 
+    xs_2[x] = added(copies_2, p2_2[y], r2_2)
+    copies_2 = [remote(xs_2.at[x], xs_2.at[x], 187 + k, peers_x[k - 1], landed=183 + x) for k in range(1, XS)]
+    for copy in copies_2:
+        send(copy)
     back_first.wait_recv()
     back_last.wait_recv()
 
@@ -551,6 +574,11 @@
     store = pltpu.make_async_copy(gs, ig_out.at[0], local_sem.at[16])
     store.start()
 
+    for k in range(1, XS):
+        src = (x + k) % XS
+        remote(xs_2.at[src], xs_2.at[src], 187, partner, landed=183 + src).wait_recv()
+    f_2[zlo] = sum(xs_2[k].astype(F32) for k in range(XS)).astype(BF16)
+    swap_z = send(remote(f_2.at[zlo], f_2.at[zlo], 191, at(tm_=(1 - zlo) * XS + x)))
     f_x[tm] = added(z_copies, zs_x[zlo, dp], zr_x)
     for k in range(1, TM):
         send(remote(f_x.at[tm], f_x.at[tm], 163 + k, peers_tm[k - 1]))
@@ -561,23 +589,24 @@
         remote(f_x.at[src], f_x.at[src], 163 + k, at(tm_=src)).wait_recv()
     for wait in last_waits:
         wait()
-    time0_out[...], time1_out[...], down_out[...] = f_0[...], f_1[...], f_x[...]
+    swap_z.wait_recv()
+    time0_out[...], time1_out[...], time2_out[...], down_out[...] = f_0[...], f_1[...], f_2[...], f_x[...]
 
     for copy in sent:
         copy.wait_send()
-    for ring in (ring_0, ring_1, ring_x):
-        ring.finish()
+    ring_x.finish()
     store.wait()
 
 
-def finish(ig, time0, time1, down, ig_out, time_out, down_out, held, load_sem, store_sem):
+def finish(ig, time0, time1, time2, down, ig_out, time_out, down_out, held, load_sem, store_sem):
     loads = [pltpu.make_async_copy(ig.at[0, t], held.at[t], load_sem.at[t]) for t in range(FINE)]
     stores = [pltpu.make_async_copy(held.at[t], ig_out.at[0, t], store_sem.at[t]) for t in range(FINE)]
     for load in loads:
         load.start()
     odd = lax.axis_index("dp") % 2 == 1
     scale = 1.0 / math.sqrt(ROWS_ALL)
-    rows = jnp.concatenate([time0[...], time1[...]], axis=2).astype(F32).reshape(64, C1) * scale
+    pieces = [time[...].astype(F32).reshape(64, -1) for time in (time0, time1, time2)]
+    rows = jnp.concatenate(pieces, axis=1) * scale
     time_out[...] = jnp.where(odd, rows[4:64], rows[:60])
     halves = [down[half * XS + part_x] for part_x in range(XS) for half in range(2)]
     wide = jnp.concatenate(halves, axis=1).astype(F32) * (0.25 * scale)
@@ -594,7 +623,7 @@
     v = pltpu.VMEM
     return [
         v((YS, DP, 64, n), BF16), v((YS, DP, 64, n), BF16),
-        v((2, 64, n), BF16), v((2, 64, n), BF16), v((4, 64, n), BF16), v((4, 64, n), BF16),
+        v((YS - 1, DP, 64, n), BF16),
         v((XS, DP, 16, n), BF16), v((XS - 1, DP, 16, n), BF16),
         v((DP, 16, n), BF16), v((2 * DP, 16, n), BF16), v((XS, 16, n), BF16),
     ]
@@ -604,9 +633,17 @@
     v = pltpu.VMEM
     return [
         v((XS, YS, DP, 16, n), BF16), v((XS, YS, DP, 16, n), BF16),
-        v((2, DP, 16, n), BF16), v((2, DP, 16, n), BF16), v((4, DP, 16, n), BF16), v((4, DP, 16, n), BF16),
+        v((XS - 1, YS, DP, 16, n), BF16),
         v((YS, DP, 16, n), BF16), v((YS - 1, DP, 16, n), BF16),
         v((DP, 16, n), BF16), v((2 * DP, 16, n), BF16), v((XS, 16, n), BF16),
+    ]
+
+
+def first_over_z(n):
+    v = pltpu.VMEM
+    return [
+        v((DP, 2, YS, 32, n), BF16), v((DP, 2, YS, 32, n), BF16), v((7, YS, 32, n), BF16),
+        v((YS, 32, n), BF16), v((YS - 1, 32, n), BF16), v((XS, 32, n), BF16), v((2, 32, n), BF16),
     ]
 
 
@@ -622,22 +659,24 @@
         v((PIX, C1), BF16), v((PIX, C2), BF16), v((PIX, C1), F32), v((FINE + 2, PIX, C1), BF16),
         v((3 * C1, C1), F32), v((C1, C2), F32),
         *first_over_y(PIECES[0][1] - PIECES[0][0]), *first_over_x(PIECES[1][1] - PIECES[1][0]),
+        *first_over_z(PIECES[2][1] - PIECES[2][0]),
         v((XS, YS, DP, 16, DC), BF16), v((XS, YS, DP, 16, DC), BF16),
         *[v((2, DP, 16, DC), BF16)] * 2, *[v((4, DP, 16, DC), BF16)] * 2,
         v((YS, DP, 16, DC), BF16), v((YS - 1, DP, 16, DC), BF16),
         v((2, DP, 16, DC // 2), BF16), v((7, 16, DC // 2), BF16), v((TM, 16, DC // 2), BF16),
-        pltpu.SemaphoreType.DMA((17,)), pltpu.SemaphoreType.DMA((171,)), pltpu.SemaphoreType.DMA((171,)),
+        pltpu.SemaphoreType.DMA((17,)), pltpu.SemaphoreType.DMA((192,)), pltpu.SemaphoreType.DMA((192,)),
     ]
     fine = jax.ShapeDtypeStruct((1, FINE, PIX, C1), BF16)
     ig, *sums = pl.pallas_call(
         kernel,
         out_shape=(
             fine,
-            *[jax.ShapeDtypeStruct((XS, 16, hi - lo), BF16) for lo, hi in PIECES],
+            *[jax.ShapeDtypeStruct((XS, 16, hi - lo), BF16) for lo, hi in PIECES[:2]],
+            jax.ShapeDtypeStruct((2, 32, PIECES[2][1] - PIECES[2][0]), BF16),
             jax.ShapeDtypeStruct((TM, 16, DC // 2), BF16),
         ),
         in_specs=[hbm] * 7,
-        out_specs=(hbm, vmem, vmem, vmem),
+        out_specs=(hbm, vmem, vmem, vmem, vmem),
         scratch_shapes=scratch,
         compiler_params=pltpu.CompilerParams(
             collective_id=0, has_side_effects=True, vmem_limit_bytes=60 * 1024 * 1024
@@ -647,7 +686,7 @@
     return pl.pallas_call(
         finish,
         out_shape=(fine, jax.ShapeDtypeStruct((60, C1), F32), jax.ShapeDtypeStruct((20, C2), F32)),
-        in_specs=[hbm, vmem, vmem, vmem],
+        in_specs=[hbm, vmem, vmem, vmem, vmem],
         out_specs=(hbm, vmem, vmem),
         scratch_shapes=[
             v((FINE, PIX, C1), BF16),

time: 78.3 us -> 78.6 us (level)
  no operation moved by 1% of the time
where the time goes in v6:
time: 78.6 us; the launch traced here: 78.1 us
  Pallas kernels  77.3 us (98%)
  between operations  0.8 us (1%)
    pallas_call x1, Pallas kernels, shards(): pl.pallas_call(kernel, out_shape=(fine, *[jax.ShapeDtypeStruct((XS, 16, h...  73.6 us
    pallas_call x1, Pallas kernels, shards(): pl.pallas_call(finish, out_shape=(fine, jax.ShapeDtypeStruct((60, C1), F3...  3.67 us

profile of v6, /device:TPU:2, one launch (start us, length us, event | category | flops | bytes accessed | tf_op | source)
XLA Modules:
  0.0 78.1 jit_solution(15158324949527007922)
XLA Ops:
  0.6 73.6 %shard_map.94 = (bf16[1,4,192,640]{3,2,1,0:T(8,128)(2,1)}, bf16[4,16,256]{2,1,0:T(8,128)(2,1)}, bf16[4,16,256]{2,1,0:T(8,128)(2,1)}, bf16[2,32,128]{2,1,0:T(8,128)(2,1)}, bf16[8,16,256]{2,1,0:T(8,128)(2,1)}) custom-call(bf16[1,4,192,640]{3,2,1,0:T(8,128)(2,1)} %frames.1, bf16[1920,640]{1,0:T(8,128)(2,1)} %w_time.1, bf16[640,1280]{1,0:T(8,128)(2,1)} %w_down.1, ...), custom_call_target="tpu_custom_call" | custom-call | flops 8999999488 | bytes 16000000 | tf_op jit(solution)/shard_map/pallas_call | solution.py:670
  74.2 3.7 %shard_map.95 = (bf16[1,4,192,640]{3,2,1,0:T(8,128)(2,1)}, f32[60,640]{1,0:T(8,128)}, f32[20,1280]{1,0:T(8,128)}) custom-call(bf16[1,4,192,640]{3,2,1,0:T(8,128)(2,1)} %get-tuple-element.8.ig, bf16[4,16,256]{2,1,0:T(8,128)(2,1)} %get-tuple-element.9.time0, bf16[4,16,256]{2,1,0:T(8,128)(2,1)} %get-tuple-element.10.time1, ...), custom_call_target="tpu_custom_call" | custom-call | flops 100000 | bytes 2000000 | tf_op jit(solution)/shard_map/pallas_call | solution.py:686

commit v7 on v6

--- a/solution.py
+++ b/solution.py
@@ -361,7 +361,7 @@
         for h in range(DP):
             unit = down_unit(part_y, 1 - core, h).astype(BF16)
             for part_x in range(XS):
-                cs_x[part_x, part_y, h] = unit[:, DC * part_x : DC * part_x + DC]
+                cs_x[part_y, part_x, h] = unit[:, DC * part_x : DC * part_x + DC]
         return carry
 
     def add_down(part_y, carry):
@@ -369,15 +369,15 @@
             unit = down_unit(part_y, core, h)
             for part_x in range(XS):
                 more = unit[:, DC * part_x : DC * part_x + DC]
-                p_x[part_x, part_y, h] = (p_x[part_x, part_y, h].astype(F32) + more).astype(BF16)
+                p_x[part_y, part_x, h] = (p_x[part_y, part_x, h].astype(F32) + more).astype(BF16)
         return carry
 
     lax.fori_loop(0, YS, pack_down, 0)
     swap_x = send(remote(cs_x, p_x, 106, partner))
     swap_x.wait_recv()
     lax.fori_loop(0, YS, add_down, 0)
-    ring_x = Ring(remote, p_x, (x_ra, x_rb, x_fp, x_fm), x, peers_x[0], peers_x[2], 92)
-    ring_x.start()
+    ring_d = Ring(remote, p_x, (x_ra, x_rb, x_fp, x_fm), y, peers_y[0], peers_y[2], 92)
+    ring_d.start()
 
     loads[6].wait()
     for c in range(CHUNKS):
@@ -387,6 +387,9 @@
         for t in range(FINE):
             back = gs[t, :, lo:hi].astype(F32) + spread[:, lo:hi]
             bpe[t + 1, :, lo:hi] = (back * pre[t, :, lo:hi]).astype(BF16)
+
+    back_first = send(remote(bpe.at[1], bpe.at[FINE + 1], 78, prev))
+    back_last = send(remote(bpe.at[FINE], bpe.at[0], 79, nxt))
 
     def time_grad(piece, cs, parts, place, shape):
         left, right = PIECES[piece]
@@ -421,7 +424,7 @@
         return (h, slice(None), part_y)
 
     time_grad(0, cs_0, p_0, by_y, (64,))
-    ring_x.middle()
+    ring_d.middle()
     time_grad(1, cs_1, p_1, by_x, (XS, 16))
     copies_0 = []
     for k in (2, 1, 3, 0):
@@ -460,12 +463,29 @@
         return (own.astype(F32) + sum(more[k].astype(F32) for k in range(len(copies)))).astype(BF16)
 
     input_grad(1, 2, *COLS_FINE[0])
-    ring_x.arrived()
-    for part_y in range(YS):
-        p2_x[part_y] = ring_x.total(part_y).astype(BF16)
-    copies_x = [send(remote(p2_x.at[(y + k) % YS], r2_x.at[k - 1], 113 + k, peers_y[k - 1])) for k in range(1, YS)]
+    ring_d.arrived()
+    for part_x in range(XS):
+        p2_x[part_x] = ring_d.total(part_x).astype(BF16)
+    copies_x = [send(remote(p2_x.at[(x + k) % XS], r2_x.at[k - 1], 113 + k, peers_x[k - 1])) for k in range(1, XS)]
     input_grad(1, 2, *COLS_FINE[1])
     input_grad(1, 2, *COLS_FINE[2])
+    back_first.wait_recv()
+    back_last.wait_recv()
+
+    @pl.when(tm == 0)
+    def _():
+        bpe[0] = jnp.zeros((PIX, C1), BF16)
+
+    @pl.when(tm == TM - 1)
+    def _():
+        bpe[FINE + 1] = jnp.zeros((PIX, C1), BF16)
+
+    for lo, hi in COLS_FINE:
+        input_grad(0, 1, lo, hi)
+        input_grad(3, 1, lo, hi)
+    store = pltpu.make_async_copy(gs, ig_out.at[0], local_sem.at[16])
+    store.start()
+
     arrived(copies_0)
     for h in range(DP):
         total = p_0[y, h].astype(F32) + sum(r_0[k, h].astype(F32) for k in range(YS - 1))
@@ -475,8 +495,6 @@
     for part_y in range(YS):
         p2_1[part_y] = (p_1[x, part_y].astype(F32) + sum(r_1[k, part_y].astype(F32) for k in range(XS - 1))).astype(BF16)
     copies_1 = [send(remote(p2_1.at[(y + k) % YS], r2_1.at[k - 1], 110 + k, peers_y[k - 1])) for k in range(1, YS)]
-    back_first = send(remote(bpe.at[1], bpe.at[FINE + 1], 78, prev))
-    back_last = send(remote(bpe.at[FINE], bpe.at[0], 79, nxt))
     p2_2[...] = added(copies_2, p_2[dp, zlo], zr_2)
     copies_2 = [send(remote(p2_2.at[(y + k) % YS], r2_2.at[k - 1], 177 + k, peers_y[k - 1])) for k in range(1, YS)]
 
@@ -542,7 +560,7 @@
 
             last_waits.append(finish)
 
-    sums = added(copies_x, p2_x[y], r2_x)
+    sums = added(copies_x, p2_x[x], r2_x)
     for half in range(2):
         zs_x[half] = sums[:, :, half * DC // 2 : (half + 1) * DC // 2]
     z_copies = [
@@ -557,22 +575,6 @@
     copies_2 = [remote(xs_2.at[x], xs_2.at[x], 187 + k, peers_x[k - 1], landed=183 + x) for k in range(1, XS)]
     for copy in copies_2:
         send(copy)
-    back_first.wait_recv()
-    back_last.wait_recv()
-
-    @pl.when(tm == 0)
-    def _():
-        bpe[0] = jnp.zeros((PIX, C1), BF16)
-
-    @pl.when(tm == TM - 1)
-    def _():
-        bpe[FINE + 1] = jnp.zeros((PIX, C1), BF16)
-
-    for lo, hi in COLS_FINE:
-        input_grad(0, 1, lo, hi)
-        input_grad(3, 1, lo, hi)
-    store = pltpu.make_async_copy(gs, ig_out.at[0], local_sem.at[16])
-    store.start()
 
     for k in range(1, XS):
         src = (x + k) % XS
@@ -594,7 +596,7 @@
 
     for copy in sent:
         copy.wait_send()
-    ring_x.finish()
+    ring_d.finish()
     store.wait()
 
 

time: 78.6 us -> 75.9 us (0.966)
  Pallas kernels: 77.3 us -> 74.4 us
    pallas_call x1, Pallas kernels: 73.6 us -> 70.7 us  [shards(): pl.pallas_call(kernel, out_shape=(fine, *[jax.ShapeDtypeStruct((XS, 16, h...]
where the time goes in v7:
time: 75.9 us; the launch traced here: 75.2 us
  Pallas kernels  74.4 us (98%)
  between operations  0.82 us (1%)
    pallas_call x1, Pallas kernels, shards(): pl.pallas_call(kernel, out_shape=(fine, *[jax.ShapeDtypeStruct((XS, 16, h...  70.7 us
    pallas_call x1, Pallas kernels, shards(): pl.pallas_call(finish, out_shape=(fine, jax.ShapeDtypeStruct((60, C1), F3...  3.67 us

profile of v7, /device:TPU:2, one launch (start us, length us, event | category | flops | bytes accessed | tf_op | source)
XLA Modules:
  0.0 75.2 jit_solution(2815938001454167872)
XLA Ops:
  0.6 70.7 %shard_map.94 = (bf16[1,4,192,640]{3,2,1,0:T(8,128)(2,1)}, bf16[4,16,256]{2,1,0:T(8,128)(2,1)}, bf16[4,16,256]{2,1,0:T(8,128)(2,1)}, bf16[2,32,128]{2,1,0:T(8,128)(2,1)}, bf16[8,16,256]{2,1,0:T(8,128)(2,1)}) custom-call(bf16[1,4,192,640]{3,2,1,0:T(8,128)(2,1)} %frames.1, bf16[1920,640]{1,0:T(8,128)(2,1)} %w_time.1, bf16[640,1280]{1,0:T(8,128)(2,1)} %w_down.1, ...), custom_call_target="tpu_custom_call" | custom-call | flops 8999999488 | bytes 16000000 | tf_op jit(solution)/shard_map/pallas_call | solution.py:672
  71.4 3.7 %shard_map.95 = (bf16[1,4,192,640]{3,2,1,0:T(8,128)(2,1)}, f32[60,640]{1,0:T(8,128)}, f32[20,1280]{1,0:T(8,128)}) custom-call(bf16[1,4,192,640]{3,2,1,0:T(8,128)(2,1)} %get-tuple-element.8.ig, bf16[4,16,256]{2,1,0:T(8,128)(2,1)} %get-tuple-element.9.time0, bf16[4,16,256]{2,1,0:T(8,128)(2,1)} %get-tuple-element.10.time1, ...), custom_call_target="tpu_custom_call" | custom-call | flops 100000 | bytes 2000000 | tf_op jit(solution)/shard_map/pallas_call | solution.py:688

commit v8 on v7

--- a/solution.py
+++ b/solution.py
@@ -424,8 +424,8 @@
         return (h, slice(None), part_y)
 
     time_grad(0, cs_0, p_0, by_y, (64,))
+    time_grad(1, cs_1, p_1, by_x, (XS, 16))
     ring_d.middle()
-    time_grad(1, cs_1, p_1, by_x, (XS, 16))
     copies_0 = []
     for k in (2, 1, 3, 0):
         part_y = (y + k) % YS

time: 75.9 us -> 76 us (level)
  no operation moved by 1% of the time
where the time goes in v8:
time: 76 us; the launch traced here: 75.8 us
  Pallas kernels  75 us (99%)
  between operations  0.82 us (1%)
    pallas_call x1, Pallas kernels, shards(): pl.pallas_call(kernel, out_shape=(fine, *[jax.ShapeDtypeStruct((XS, 16, h...  71.3 us
    pallas_call x1, Pallas kernels, shards(): pl.pallas_call(finish, out_shape=(fine, jax.ShapeDtypeStruct((60, C1), F3...  3.67 us

profile of v8, /device:TPU:2, one launch (start us, length us, event | category | flops | bytes accessed | tf_op | source)
XLA Modules:
  0.0 75.8 jit_solution(11417546249148888932)
XLA Ops:
  0.6 71.3 %shard_map.94 = (bf16[1,4,192,640]{3,2,1,0:T(8,128)(2,1)}, bf16[4,16,256]{2,1,0:T(8,128)(2,1)}, bf16[4,16,256]{2,1,0:T(8,128)(2,1)}, bf16[2,32,128]{2,1,0:T(8,128)(2,1)}, bf16[8,16,256]{2,1,0:T(8,128)(2,1)}) custom-call(bf16[1,4,192,640]{3,2,1,0:T(8,128)(2,1)} %frames.1, bf16[1920,640]{1,0:T(8,128)(2,1)} %w_time.1, bf16[640,1280]{1,0:T(8,128)(2,1)} %w_down.1, ...), custom_call_target="tpu_custom_call" | custom-call | flops 8999999488 | bytes 16000000 | tf_op jit(solution)/shard_map/pallas_call | solution.py:672
  71.9 3.7 %shard_map.95 = (bf16[1,4,192,640]{3,2,1,0:T(8,128)(2,1)}, f32[60,640]{1,0:T(8,128)}, f32[20,1280]{1,0:T(8,128)}) custom-call(bf16[1,4,192,640]{3,2,1,0:T(8,128)(2,1)} %get-tuple-element.8.ig, bf16[4,16,256]{2,1,0:T(8,128)(2,1)} %get-tuple-element.9.time0, bf16[4,16,256]{2,1,0:T(8,128)(2,1)} %get-tuple-element.10.time1, ...), custom_call_target="tpu_custom_call" | custom-call | flops 100000 | bytes 2000000 | tf_op jit(solution)/shard_map/pallas_call | solution.py:688
